TPU v7x, 256 devices: a whole 4x4x8 slice. The times are simulated.
256 devices in a mesh: group: 8 (over z), shard: 32 (over y, x, core).
Axes of the slice: x: 4, y: 4, z: 8, core: 2. Of those that a mesh axis runs over, the one named last changes fastest.
Arguments:
- queries: bfloat16 [4096, 32, 128], P(('group', 'shard')), parts along dimension 0, may hold values from -6 to 6
- passages: bfloat16 [4096, 180, 128], P('shard'), may hold values from -6 to 6
- lengths: int32 [4096], P('shard'), may hold values from 8 to 180
- candidates: int32 [4096, 64], P(('group', 'shard')), parts along dimension 0, may hold values from 0 to 4095, as said below
Outputs:
- scores: float32 [4096, 64], P(('group', 'shard')), parts along dimension 0
There are 8 independent parts, one for each index of `group`. A program takes and returns all parts, laid end to end along the dimension named above; an argument that names none is the same for every part. Nothing has to cross between parts.
Inputs may be any that keep to these rules, and one draw needn't show every extreme that they name: Candidate ids of one query are distinct. For the queries of one device (aligned blocks of 16 rows) at most 96 candidates fall in the block of 128 passages of any one device, and exactly 96 fall in one such block.
All inputs are finite; a program needn't handle non-finite values.
Results may differ from a plain program's by a relative error of at most 0.0003.
Values may be sent and summed in bfloat16 or wider, within the bound.
A program may use at most 128 MiB of HBM per device.

v0:
```python
import jax
import jax.numpy as jnp
from jax import lax
from jax.sharding import PartitionSpec as P


def shards(queries, passages, lengths, candidates):
    shard_count = lax.axis_size("shard")
    my_index = lax.axis_index("shard")
    pass_local = passages.shape[0]
    plen_local = passages.shape[1]
    query_count, cand_count = candidates.shape
    qtok_local = queries.shape[1]
    dim_local = queries.shape[2]
    pair_count = query_count * cand_count
    capacity = 3 * pair_count // shard_count
    highest = lax.Precision.HIGHEST
    cap_slots = jnp.arange(capacity, dtype=jnp.int32)
    all_lists = lax.all_gather(candidates, "shard", axis=0, tiled=True)
    all_lists = all_lists.reshape(shard_count, pair_count)
    local_hit = (all_lists // pass_local == my_index).astype(jnp.int32)
    hit_rank = jnp.cumsum(local_hit, axis=1) - local_hit
    all_codes = (
        jnp.arange(pair_count, dtype=jnp.int32)[None, :] * pass_local + all_lists % pass_local
    )
    place = jnp.logical_and(
        hit_rank[:, :, None] == cap_slots[None, None, :], local_hit[:, :, None] > 0
    ).astype(jnp.float32)
    code_sum = jnp.einsum("sn,snk->sk", all_codes.astype(jnp.float32), place, precision=highest)
    filled = jnp.sum(place, axis=1)
    received = jnp.where(filled > 0.5, code_sum.astype(jnp.int32), -1)
    all_queries = lax.all_gather(queries, "shard", axis=0, tiled=True)
    alive_slot = received >= 0
    safe_code = jnp.maximum(received, 0)
    pair_index = safe_code // pass_local
    local_query = pair_index // cand_count
    passage_index = safe_code % pass_local
    merged = max(1, shard_count // 16)
    rounds = shard_count // merged
    token_slots = jnp.arange(plen_local, dtype=jnp.int32)
    query_slots = jnp.arange(query_count, dtype=jnp.int32)
    pass_slots = jnp.arange(pass_local, dtype=jnp.int32)
    query_table = all_queries.reshape(rounds, merged, query_count, qtok_local * dim_local)
    passage_flat = passages.reshape(pass_local, plen_local * dim_local)

    def score_block(block_args):
        table, query_ids, passage_ids, alive_ids = block_args
        pick = (query_ids[:, :, None] == query_slots[None, None, :]).astype(jnp.bfloat16)
        query_block = jnp.einsum(
            "mcq,mqf->mcf", pick, table, preferred_element_type=jnp.float32
        ).astype(jnp.bfloat16)
        query_block = query_block.reshape(-1, qtok_local, dim_local)
        flat_pass = passage_ids.reshape(-1)
        passage_block = jnp.take(passage_flat, flat_pass, axis=0).reshape(-1, plen_local, dim_local)
        live_len = jnp.sum(
            jnp.where(flat_pass[:, None] == pass_slots[None, :], lengths[None, :], 0), axis=1
        )
        similar = jnp.einsum(
            "bid,btd->bit", query_block, passage_block, preferred_element_type=jnp.float32
        )
        inside = token_slots[None, None, :] < live_len[:, None, None]
        best_match = jnp.max(jnp.where(inside, similar, jnp.float32(-1e30)), axis=2)
        return jnp.where(alive_ids.reshape(-1), jnp.mean(best_match, axis=1), jnp.float32(0.0))

    scores = lax.map(
        score_block,
        (
            query_table,
            local_query.reshape(rounds, merged, capacity),
            passage_index.reshape(rounds, merged, capacity),
            alive_slot.reshape(rounds, merged, capacity),
        ),
    )
    scores = scores.reshape(shard_count, capacity)
    pair_slots = jnp.arange(pair_count, dtype=jnp.int32)
    spread = jnp.logical_and(
        pair_index[:, :, None] == pair_slots[None, None, :], alive_slot[:, :, None]
    ).astype(jnp.float32)
    dense_rows = jnp.einsum("sk,skn->sn", scores, spread, precision=highest)
    result = lax.psum_scatter(
        dense_rows.reshape(shard_count * query_count, cand_count),
        "shard",
        scatter_dimension=0,
        tiled=True,
    )
    return result


def solution(mesh):
    in_specs = (
        P(("group", "shard"), None, None),
        P("shard", None, None),
        P("shard"),
        P(("group", "shard"), None),
    )
    out_specs = P(("group", "shard"), None)
    return jax.shard_map(shards, mesh=mesh, in_specs=in_specs, out_specs=out_specs, check_vma=False)
```

profile of v0, /device:TPU:1, one launch (start us, length us, event | category | flops | bytes accessed | tf_op | source)
XLA Modules:
  0.0 897.5 jit_solution(14843078470470422948)
XLA Ops:
  7.3 26.4 %all_gather.6 = s32[512,64]{1,0:T(8,128)S(1)} all-gather(s32[16,64]{1,0:T(8,128)} %param.9), channel_id=1, replica_groups=mesh['group'=8,'shard'=32] {'shard'}, dimensions={0}, use_global_device_ids=true | all-gather | bytes 135168 | tf_op jit(solution)/shard_map/all_gather | solution.py:19
  77.6 724.4 %while.11 = (s32[]{:T(128)}, f32[16,192]{1,0:T(8,128)S(1)}, pred[16,2,96]{2,1,0:T(4,128)(4,1)S(1)}, s32[16,2,96]{2,1,0:T(2,128)S(1)}, s32[128]{0:T(128)S(1)}, /*...) while((s32[]{:T(128)}, f32[16,192]{1,0:T(8,128)S(1)}, ...), condition=%wide.region_7.8_spmd.clone, body=%wide.region_3.7_spmd.clone.sunk | while | flops 315817408 | bytes 50933696 | solution.py:65
  80.2 20.6 %gather_fusion = bf16[192,23040]{1,0:T(8,128)(2,1)} fusion(bf16[128,23040]{1,0:T(8,128)(2,1)} %get-tuple-element.214, s32[1024]{0:T(1024)S(1)} %pad_clamp_fusion.2), kind=kCustom, calls=%fused_computation.clone.clone.1 | custom fusion | bytes 17695488 | tf_op jit(solution)/shard_map/while/body/eval_jaxpr/jit(_take)/gather | solution.py:54
  125.4 20.6 %gather_fusion = bf16[192,23040]{1,0:T(8,128)(2,1)} fusion(bf16[128,23040]{1,0:T(8,128)(2,1)} %get-tuple-element.214, s32[1024]{0:T(1024)S(1)} %pad_clamp_fusion.2), kind=kCustom, calls=%fused_computation.clone.clone.1 | custom fusion | bytes 17695488 | tf_op jit(solution)/shard_map/while/body/eval_jaxpr/jit(_take)/gather | solution.py:54
  146.1 12.7 %gather.13 = bf16[192,180,128]{2,1,0:T(8,128)(2,1)} reshape(bf16[192,23040]{1,0:T(8,128)(2,1)} %gather_fusion) | data formatting | bytes 17694720 | tf_op jit(solution)/shard_map/while/body/eval_jaxpr/jit(_take)/gather | solution.py:54
  170.7 20.6 %gather_fusion = bf16[192,23040]{1,0:T(8,128)(2,1)} fusion(bf16[128,23040]{1,0:T(8,128)(2,1)} %get-tuple-element.214, s32[1024]{0:T(1024)S(1)} %pad_clamp_fusion.2), kind=kCustom, calls=%fused_computation.clone.clone.1 | custom fusion | bytes 17695488 | tf_op jit(solution)/shard_map/while/body/eval_jaxpr/jit(_take)/gather | solution.py:54
  191.3 12.7 %gather.13 = bf16[192,180,128]{2,1,0:T(8,128)(2,1)} reshape(bf16[192,23040]{1,0:T(8,128)(2,1)} %gather_fusion) | data formatting | bytes 17694720 | tf_op jit(solution)/shard_map/while/body/eval_jaxpr/jit(_take)/gather | solution.py:54
  216.0 20.6 %gather_fusion = bf16[192,23040]{1,0:T(8,128)(2,1)} fusion(bf16[128,23040]{1,0:T(8,128)(2,1)} %get-tuple-element.214, s32[1024]{0:T(1024)S(1)} %pad_clamp_fusion.2), kind=kCustom, calls=%fused_computation.clone.clone.1 | custom fusion | bytes 17695488 | tf_op jit(solution)/shard_map/while/body/eval_jaxpr/jit(_take)/gather | solution.py:54
  261.2 20.6 %gather_fusion = bf16[192,23040]{1,0:T(8,128)(2,1)} fusion(bf16[128,23040]{1,0:T(8,128)(2,1)} %get-tuple-element.214, s32[1024]{0:T(1024)S(1)} %pad_clamp_fusion.2), kind=kCustom, calls=%fused_computation.clone.clone.1 | custom fusion | bytes 17695488 | tf_op jit(solution)/shard_map/while/body/eval_jaxpr/jit(_take)/gather | solution.py:54
  306.5 20.6 %gather_fusion = bf16[192,23040]{1,0:T(8,128)(2,1)} fusion(bf16[128,23040]{1,0:T(8,128)(2,1)} %get-tuple-element.214, s32[1024]{0:T(1024)S(1)} %pad_clamp_fusion.2), kind=kCustom, calls=%fused_computation.clone.clone.1 | custom fusion | bytes 17695488 | tf_op jit(solution)/shard_map/while/body/eval_jaxpr/jit(_take)/gather | solution.py:54
  327.1 12.7 %gather.13 = bf16[192,180,128]{2,1,0:T(8,128)(2,1)} reshape(bf16[192,23040]{1,0:T(8,128)(2,1)} %gather_fusion) | data formatting | bytes 17694720 | tf_op jit(solution)/shard_map/while/body/eval_jaxpr/jit(_take)/gather | solution.py:54
  351.7 20.6 %gather_fusion = bf16[192,23040]{1,0:T(8,128)(2,1)} fusion(bf16[128,23040]{1,0:T(8,128)(2,1)} %get-tuple-element.214, s32[1024]{0:T(1024)S(1)} %pad_clamp_fusion.2), kind=kCustom, calls=%fused_computation.clone.clone.1 | custom fusion | bytes 17695488 | tf_op jit(solution)/shard_map/while/body/eval_jaxpr/jit(_take)/gather | solution.py:54
  397.0 20.6 %gather_fusion = bf16[192,23040]{1,0:T(8,128)(2,1)} fusion(bf16[128,23040]{1,0:T(8,128)(2,1)} %get-tuple-element.214, s32[1024]{0:T(1024)S(1)} %pad_clamp_fusion.2), kind=kCustom, calls=%fused_computation.clone.clone.1 | custom fusion | bytes 17695488 | tf_op jit(solution)/shard_map/while/body/eval_jaxpr/jit(_take)/gather | solution.py:54
  442.3 20.6 %gather_fusion = bf16[192,23040]{1,0:T(8,128)(2,1)} fusion(bf16[128,23040]{1,0:T(8,128)(2,1)} %get-tuple-element.214, s32[1024]{0:T(1024)S(1)} %pad_clamp_fusion.2), kind=kCustom, calls=%fused_computation.clone.clone.1 | custom fusion | bytes 17695488 | tf_op jit(solution)/shard_map/while/body/eval_jaxpr/jit(_take)/gather | solution.py:54
  462.9 12.7 %gather.13 = bf16[192,180,128]{2,1,0:T(8,128)(2,1)} reshape(bf16[192,23040]{1,0:T(8,128)(2,1)} %gather_fusion) | data formatting | bytes 17694720 | tf_op jit(solution)/shard_map/while/body/eval_jaxpr/jit(_take)/gather | solution.py:54
  487.5 20.6 %gather_fusion = bf16[192,23040]{1,0:T(8,128)(2,1)} fusion(bf16[128,23040]{1,0:T(8,128)(2,1)} %get-tuple-element.214, s32[1024]{0:T(1024)S(1)} %pad_clamp_fusion.2), kind=kCustom, calls=%fused_computation.clone.clone.1 | custom fusion | bytes 17695488 | tf_op jit(solution)/shard_map/while/body/eval_jaxpr/jit(_take)/gather | solution.py:54
  508.2 12.7 %gather.13 = bf16[192,180,128]{2,1,0:T(8,128)(2,1)} reshape(bf16[192,23040]{1,0:T(8,128)(2,1)} %gather_fusion) | data formatting | bytes 17694720 | tf_op jit(solution)/shard_map/while/body/eval_jaxpr/jit(_take)/gather | solution.py:54
  532.8 20.6 %gather_fusion = bf16[192,23040]{1,0:T(8,128)(2,1)} fusion(bf16[128,23040]{1,0:T(8,128)(2,1)} %get-tuple-element.214, s32[1024]{0:T(1024)S(1)} %pad_clamp_fusion.2), kind=kCustom, calls=%fused_computation.clone.clone.1 | custom fusion | bytes 17695488 | tf_op jit(solution)/shard_map/while/body/eval_jaxpr/jit(_take)/gather | solution.py:54
  578.1 20.6 %gather_fusion = bf16[192,23040]{1,0:T(8,128)(2,1)} fusion(bf16[128,23040]{1,0:T(8,128)(2,1)} %get-tuple-element.214, s32[1024]{0:T(1024)S(1)} %pad_clamp_fusion.2), kind=kCustom, calls=%fused_computation.clone.clone.1 | custom fusion | bytes 17695488 | tf_op jit(solution)/shard_map/while/body/eval_jaxpr/jit(_take)/gather | solution.py:54
  623.3 20.6 %gather_fusion = bf16[192,23040]{1,0:T(8,128)(2,1)} fusion(bf16[128,23040]{1,0:T(8,128)(2,1)} %get-tuple-element.214, s32[1024]{0:T(1024)S(1)} %pad_clamp_fusion.2), kind=kCustom, calls=%fused_computation.clone.clone.1 | custom fusion | bytes 17695488 | tf_op jit(solution)/shard_map/while/body/eval_jaxpr/jit(_take)/gather | solution.py:54
  668.6 20.6 %gather_fusion = bf16[192,23040]{1,0:T(8,128)(2,1)} fusion(bf16[128,23040]{1,0:T(8,128)(2,1)} %get-tuple-element.214, s32[1024]{0:T(1024)S(1)} %pad_clamp_fusion.2), kind=kCustom, calls=%fused_computation.clone.clone.1 | custom fusion | bytes 17695488 | tf_op jit(solution)/shard_map/while/body/eval_jaxpr/jit(_take)/gather | solution.py:54
  713.8 20.6 %gather_fusion = bf16[192,23040]{1,0:T(8,128)(2,1)} fusion(bf16[128,23040]{1,0:T(8,128)(2,1)} %get-tuple-element.214, s32[1024]{0:T(1024)S(1)} %pad_clamp_fusion.2), kind=kCustom, calls=%fused_computation.clone.clone.1 | custom fusion | bytes 17695488 | tf_op jit(solution)/shard_map/while/body/eval_jaxpr/jit(_take)/gather | solution.py:54
  759.1 20.6 %gather_fusion = bf16[192,23040]{1,0:T(8,128)(2,1)} fusion(bf16[128,23040]{1,0:T(8,128)(2,1)} %get-tuple-element.214, s32[1024]{0:T(1024)S(1)} %pad_clamp_fusion.2), kind=kCustom, calls=%fused_computation.clone.clone.1 | custom fusion | bytes 17695488 | tf_op jit(solution)/shard_map/while/body/eval_jaxpr/jit(_take)/gather | solution.py:54
  807.9 82.8 %reduce-scatter.2.cloned.1.call-done = f32[16,64]{1,0:T(8,128)} async-done(((f32[512,64]{1,0:T(8,128)}), f32[16,64]{1,0:T(8,128)}) %reduce-scatter.2.cloned.1.call-update) | async-done | bytes 4112 | tf_op jit(solution)/shard_map/reduce_scatter | solution.py:80
  (339 shorter events, 379.6 us)
Async XLA Ops:
  6.5 63.7 %all-gather.2.cloned.1.call-start = ((), (), s32[]{:S(2)}) async-start(), calls=%async_computation.1 | async-start | bytes 4325376 | tf_op jit(solution)/shard_map/all_gather | solution.py:32
  7.3 883.4 %reduce-scatter.2.cloned.1.call-start = ((), (), s32[]{:S(2)}) async-start(), calls=%async_computation.2 | async-start | bytes 270336 | tf_op jit(solution)/shard_map/reduce_scatter | solution.py:80
  52.5 8.6 copy-start.1
  69.6 8.0 copy-start.3
  77.6 724.5 %copy-start = (s32[32,96]{1,0:T(8,128)S(1)}, s32[32,96]{1,0:T(8,128)}, u32[]{:S(2)}) copy-start(s32[32,96]{1,0:T(8,128)} %get-tuple-element.132) | copy-start | bytes 36868
  77.6 724.5 %copy-start.2 = (pred[32,96]{1,0:T(8,128)(4,1)S(1)}, pred[32,96]{1,0:T(8,128)(4,1)}, u32[]{:S(2)}) copy-start(pred[32,96]{1,0:T(8,128)(4,1)} %copy-done.1) | copy-start | bytes 9220
Sparse Core Ops, SparseCore 0:
  9.9 55.3 all-gather.1
  808.0 82.6 reduce-scatter.1
where the time goes:
time: 905 us; the launch traced here: 898 us
  local copies, waits for them, and re-layouts  570 us (63%)
  matrix products  183 us (20%)
  waiting for transfers between devices  83.6 us (9%)
  blocking collectives  26.4 us (3%)
  other arithmetic  19.6 us (2%)
  between operations  13.5 us (1%)
    gather x32, local copies, waits for them, and re-layouts, score_block(): jnp.take(passage_flat, flat_pass, axis=0).reshape(-1, plen_local, dim_local)  534 us
    dot_general x16, matrix products, score_block(): jnp.einsum('bid,btd->bit', query_block, passage_block, preferred_element_...  147 us
    reduce_scatter x1, waiting for transfers between devices, shards(): lax.psum_scatter(dense_rows.reshape(shard_count * query_count, cand_count...  82.8 us
    all_gather x1, blocking collectives, shards(): all_lists = lax.all_gather(candidates, 'shard', axis=0, tiled=True)  26.4 us
    dot_general x16, matrix products, score_block(): jnp.einsum('mcq,mqf->mcf', pick, table, preferred_element_type=jnp.float32)  25 us
  transfers between devices with their start and end apart: 2, of which 1 were waited for; matrix products, arithmetic and copies ran while one was open for 4% of the time, Pallas kernels for 0%

commit v1 on v0

v1 whole, which is shorter than its diff:
```python
import functools
import jax, jax.numpy as jnp
from jax import lax
from jax.experimental import pallas as pl
from jax.experimental.pallas import tpu as pltpu
from jax.sharding import PartitionSpec as P

F32, BF16, I32 = jnp.float32, jnp.bfloat16, jnp.int32
UNROLL = 16
PASS_DEV = 128
SLOTS = 512
BOUNDS = (48, 96, 144)


def nt(a, b):
    return lax.dot_general(a, b, (((1,), (1,)), ((), ())), preferred_element_type=F32)


def score_kernel(len_smem, qall, table, len_row, passages, out, pbuf, ranks, acc, lists, lists_smem, psem, lsem):
    pcount, plen, dim = passages.shape
    qcount, qtok, _ = qall.shape
    chunk = pcount // 4
    loads = [
        pltpu.make_async_copy(passages.at[pl.ds(i * chunk, chunk)], pbuf.at[pl.ds(i * chunk, chunk)], psem.at[i])
        for i in range(4)
    ]
    for load in loads:
        load.start()
    hit = table[...]
    row = lax.broadcasted_iota(I32, (qcount, qcount), 0)
    col = lax.broadcasted_iota(I32, (qcount, qcount), 1)
    before = jnp.where(col < row, 1.0, 0.0).astype(BF16)
    rank = jnp.dot(before, hit, preferred_element_type=F32)
    count = lax.dot_general(hit, jnp.ones((qcount, pcount), BF16), (((0,), (0,)), ((), ())), preferred_element_type=F32)
    blocks = jnp.floor((count + 7.0) * 0.125)
    lens = len_row[...].astype(F32)

    def class_of(lens):
        return sum(jnp.where(lens > float(bound), 1.0, 0.0) for bound in BOUNDS)

    lens_down = jnp.transpose(jnp.broadcast_to(lens, (pcount, pcount)))
    class_down = class_of(lens_down)
    p_down = lax.broadcasted_iota(I32, (pcount, pcount), 0).astype(F32)
    p_across = lax.broadcasted_iota(I32, (pcount, pcount), 1).astype(F32)
    ahead = jnp.where(class_of(lens) * pcount + p_across < class_down * pcount + p_down, 1.0, 0.0).astype(BF16)
    base = jnp.dot(ahead, blocks.astype(BF16), preferred_element_type=F32)
    wide = SLOTS // pcount
    base_w = jnp.concatenate([base] * wide, axis=1)
    blocks_w = jnp.concatenate([blocks] * wide, axis=1)
    slot = lax.broadcasted_iota(I32, (pcount, SLOTS), 1).astype(F32)
    owner = jnp.where(jnp.logical_and(slot >= base_w, slot < base_w + blocks_w), 1.0, 0.0)
    owner_p = jnp.sum(owner * lax.broadcasted_iota(I32, (pcount, SLOTS), 0).astype(F32), axis=0, keepdims=True)
    owner_base = jnp.sum(owner * base_w, axis=0, keepdims=True)
    block_of = jnp.floor(rank * 0.125)
    place = rank - 8.0 * block_of
    keyed = jnp.concatenate([jnp.where(hit > 0, block_of, 128.0).astype(BF16), place.astype(BF16)], axis=1)
    owner_b = owner.astype(BF16)
    weights = jnp.concatenate([(owner * 8.0).astype(BF16), owner_b], axis=0)
    seen = jnp.dot(keyed, weights, preferred_element_type=F32)
    seen = seen - 8.0 * (slot[:1] - owner_base)
    ranks[...] = seen
    q_down = lax.broadcasted_iota(I32, (qcount, SLOTS), 0).astype(F32)
    for k in range(8):
        ids = jnp.sum(jnp.where(seen == float(k), q_down, 0.0), axis=0, keepdims=True)
        lists[pl.ds(k, 1), :] = jnp.clip(ids.astype(I32), 0, qcount - 1)
    lists[pl.ds(8, 1), :] = jnp.clip(owner_p.astype(I32), 0, pcount - 1)
    for c in range(len(BOUNDS) + 1):
        ends = jnp.sum(jnp.where(class_down <= float(c), blocks_w[:, :pcount], 0.0), axis=0, keepdims=True)
        lists[pl.ds(9 + c, 1), :] = jnp.concatenate([ends] * wide, axis=1).astype(I32)
    move = pltpu.make_async_copy(lists, lists_smem, lsem)
    move.start()
    move.wait()
    for load in loads:
        load.wait()

    start = 0
    for c, rows in enumerate(BOUNDS + (plen,)):
        end = lists_smem[9 + c, 0]
        down = lax.broadcasted_iota(I32, (rows, 1), 0)

        def step(i, _, start=start, rows=rows, down=down):
            for u in range(UNROLL):
                b = start + i * UNROLL + u
                p = lists_smem[8, b]
                tokens = jnp.concatenate([qall[lists_smem[k, b]] for k in range(8)], axis=0)
                similar = nt(pbuf[p, :rows], tokens)
                similar = jnp.where(down < len_smem[p], similar, -1e30)
                acc[pl.ds(b, 1), :] = jnp.max(similar, axis=0, keepdims=True)
            return 0

        lax.fori_loop(0, (end - start + UNROLL - 1) // UNROLL, step, 0)
        start = end
    best = acc[:SLOTS]
    token = lax.broadcasted_iota(I32, (8, 8 * qtok), 1)
    mean = jnp.where(token // qtok == lax.broadcasted_iota(I32, (8, 8 * qtok), 0), 1.0 / qtok, 0.0).astype(BF16)
    high = best.astype(BF16)
    scores = nt(mean, high) + nt(mean, (best - high.astype(F32)).astype(BF16))
    seen = ranks[...]
    dense = sum(jnp.where(seen == float(k), scores[k : k + 1], 0.0) for k in range(8))
    high = dense.astype(BF16)
    out[...] = nt(high, owner_b) + nt((dense - high.astype(F32)).astype(BF16), owner_b)


def score(queries, table, lengths, passages):
    pcount, plen, dim = passages.shape
    qcount, qtok, _ = queries.shape
    smem, vmem = pl.BlockSpec(memory_space=pltpu.SMEM), pl.BlockSpec(memory_space=pltpu.VMEM)
    return pl.pallas_call(
        score_kernel,
        out_shape=jax.ShapeDtypeStruct((qcount, pcount), F32),
        in_specs=[smem, vmem, vmem, vmem, pl.BlockSpec(memory_space=pl.ANY)],
        out_specs=vmem,
        scratch_shapes=[
            pltpu.VMEM((pcount, plen, dim), BF16),
            pltpu.VMEM((qcount, SLOTS), F32),
            pltpu.VMEM((SLOTS + 2 * UNROLL, 8 * qtok), F32),
            pltpu.VMEM((16, SLOTS), I32),
            pltpu.SMEM((16, SLOTS), I32),
            pltpu.SemaphoreType.DMA((4,)),
            pltpu.SemaphoreType.DMA,
        ],
        compiler_params=pltpu.CompilerParams(vmem_limit_bytes=48 << 20),
        name="score",
    )(lengths, queries, table, lengths.reshape(1, -1), passages)


SIDE = 4
MESH = pl.DeviceIdType.MESH


def meet(me, count):
    barrier = pltpu.get_barrier_semaphore()

    def tell(k, _):
        peer = lax.rem(me + k, count)
        pl.semaphore_signal(barrier, inc=1, device_id={"shard": peer}, device_id_type=MESH)
        return 0

    lax.fori_loop(1, count, tell, 0)
    return lambda: pl.semaphore_wait(barrier, count - 1)


def gather_kernel(
    count, q_ref, cand_ref, qall, table, wide, slabs, send, recv, near_send, near_recv, slab_send, slab_recv, own_sem
):
    me = lax.axis_index("shard")
    core, x, y = me % 2, (me // 2) % SIDE, me // (2 * SIDE)
    block, ids = cand_ref.shape
    part = block // 2
    sibling = me + 1 - 2 * core
    arrive = meet(me, count)
    own_copy = pltpu.make_async_copy(q_ref, qall.at[pl.ds(me * block, block)], own_sem)
    own_copy.start()

    cand = cand_ref[...]
    across = lax.broadcasted_iota(jnp.int32, (ids, PASS_DEV), 1)
    down = lax.broadcasted_iota(jnp.int32, (count, ids), 0)
    local_down = jnp.transpose((cand % PASS_DEV).astype(F32)).astype(I32)
    for q in range(block):
        by_owner = jnp.where(cand[q : q + 1] // PASS_DEV == down, 1.0, 0.0).astype(BF16)
        by_local = jnp.where(local_down[:, q : q + 1] == across, 1.0, 0.0).astype(BF16)
        wide[:, q, :] = jnp.dot(by_owner, by_local, preferred_element_type=F32)
    slabs[...] = wide[...].astype(BF16)
    arrive()

    def slab_copy(k):
        peer = lax.rem(me + k, count)
        return pltpu.make_async_remote_copy(
            src_ref=slabs.at[peer],
            dst_ref=table.at[pl.ds(me * block, block)],
            send_sem=slab_send.at[k],
            recv_sem=slab_recv.at[k],
            device_id={"shard": peer},
            device_id_type=MESH,
        )

    def each(action):
        def go(k, _):
            action(slab_copy(k))
            return 0

        lax.fori_loop(1, count, go, 0)

    each(lambda copy: copy.start())
    table[pl.ds(me * block, block), :] = slabs[me]

    def device(half, first, second):
        px, py = (first, second) if half == 0 else (second, first)
        return (lax.rem(py + SIDE, SIDE) * SIDE + lax.rem(px + SIDE, SIDE)) * 2 + core

    pos = ((x, y), (y, x))
    waits = []

    def push(half, index, first, second, piece, target, own=False):
        a, b = pos[half]
        offset = half * part + piece[0]
        start = device(half, a + first, b + second) * block + offset
        dst = qall.at[pl.ds(start, piece[1])]
        near = target is None
        copy = pltpu.make_async_remote_copy(
            src_ref=q_ref.at[pl.ds(offset, piece[1])] if own else dst,
            dst_ref=dst,
            send_sem=(near_send if near else send).at[half, index],
            recv_sem=(near_recv if near else recv).at[half, index],
            device_id={"shard": sibling if near else device(half, a + target[0], b + target[1])},
            device_id_type=MESH,
        )
        copy.start()
        waits.append(copy.wait_send)
        if near:
            waits.append(copy.wait_recv)
        return copy

    full, low, high = (0, part), (0, part // 2), (part // 2, part // 2)
    halves = (0, 1)
    a = [push(h, 0, 0, 0, full, (1, 0), True) for h in halves]
    b = [push(h, 1, 0, 0, full, (-1, 0), True) for h in halves]
    up, down_, around = {}, {}, {}

    def second_axis(h, j, offset):
        up[h, j] = push(h, 4 + 4 * j, offset, 0, full, (0, 1), j == 0)
        down_[h, j] = push(h, 5 + 4 * j, offset, 0, full, (0, -1), j == 0)

    for h in halves:
        second_axis(h, 0, 0)
    for h in halves:
        push(h, 0, 0, 0, full, None, True)
    c, d = [], []
    for h in halves:
        a[h].wait_recv()
        c.append(push(h, 2, -1, 0, low, (1, 0)))
        second_axis(h, 1, -1)
        b[h].wait_recv()
        d.append(push(h, 3, 1, 0, high, (-1, 0)))
        second_axis(h, 2, 1)
    for h in halves:
        push(h, 1, -1, 0, full, None)
        push(h, 2, 1, 0, full, None)
    for h in halves:
        c[h].wait_recv()
        d[h].wait_recv()
        second_axis(h, 3, 2)
    for h in halves:
        push(h, 3, 2, 0, full, None)
    shift = (0, -1, 1, 2)
    last = []
    for j in range(4):
        for h in halves:
            up[h, j].wait_recv()
            last.append(push(h, 6 + 4 * j, shift[j], -1, low, (0, 1)))
            push(h, 4 + 4 * j, shift[j], -1, full, None)
            down_[h, j].wait_recv()
            last.append(push(h, 7 + 4 * j, shift[j], 1, high, (0, -1)))
            push(h, 5 + 4 * j, shift[j], 1, full, None)
    for i, (j, h) in enumerate((j, h) for j in range(4) for h in halves):
        last[2 * i].wait_recv()
        last[2 * i + 1].wait_recv()
        push(h, 6 + 4 * j, shift[j], 2, full, None)
    for wait in waits:
        wait()
    each(lambda copy: copy.wait())
    own_copy.wait()


def gather(queries, candidates, count):
    block, qtok, dim = queries.shape
    vmem = pl.BlockSpec(memory_space=pltpu.VMEM)
    dma = pltpu.SemaphoreType.DMA
    return pl.pallas_call(
        functools.partial(gather_kernel, count),
        out_shape=(
            jax.ShapeDtypeStruct((count * block, qtok, dim), BF16),
            jax.ShapeDtypeStruct((count * block, PASS_DEV), BF16),
        ),
        in_specs=[vmem, vmem],
        out_specs=(vmem, vmem),
        scratch_shapes=[
            pltpu.VMEM((count, block, PASS_DEV), F32),
            pltpu.VMEM((count, block, PASS_DEV), BF16),
            dma((2, 20)),
            dma((2, 20)),
            dma((2, 20)),
            dma((2, 20)),
            dma((count,)),
            dma((count,)),
            dma,
        ],
        compiler_params=pltpu.CompilerParams(collective_id=0, has_side_effects=True, vmem_limit_bytes=24 << 20),
        name="gather",
    )(queries, candidates)


def return_kernel(count, dense, cand_ref, out, slabs, send, recv):
    me = lax.axis_index("shard")
    block, ids = cand_ref.shape
    meet(me, count)()

    def slab_copy(k):
        peer = lax.rem(me + k, count)
        return pltpu.make_async_remote_copy(
            src_ref=dense.at[pl.ds(peer * block, block)],
            dst_ref=slabs.at[me],
            send_sem=send.at[k],
            recv_sem=recv.at[k],
            device_id={"shard": peer},
            device_id_type=MESH,
        )

    def each(action):
        def go(k, _):
            action(slab_copy(k))
            return 0

        lax.fori_loop(1, count, go, 0)

    each(lambda copy: copy.start())
    slabs[me] = dense[pl.ds(me * block, block), :]
    cand = cand_ref[...]
    local = cand % PASS_DEV
    local = jnp.concatenate([local] * (PASS_DEV // ids), axis=1)
    owner = cand // PASS_DEV
    each(lambda copy: copy.wait())
    total = jnp.zeros((block, ids), F32)
    for o in range(count):
        found = jnp.take_along_axis(slabs[o], local, axis=1)[:, :ids]
        total = jnp.where(owner == o, found, total)
    out[...] = total


def give_back(dense, candidates, count):
    block, ids = candidates.shape
    vmem = pl.BlockSpec(memory_space=pltpu.VMEM)
    dma = pltpu.SemaphoreType.DMA
    return pl.pallas_call(
        functools.partial(return_kernel, count),
        out_shape=jax.ShapeDtypeStruct((block, ids), F32),
        in_specs=[vmem, vmem],
        out_specs=vmem,
        scratch_shapes=[pltpu.VMEM((count, block, PASS_DEV), F32), dma((count,)), dma((count,))],
        compiler_params=pltpu.CompilerParams(collective_id=1, has_side_effects=True),
        name="give_back",
    )(dense, candidates)


def shards(queries, passages, lengths, candidates):
    count = lax.axis_size("shard")
    every, table = gather(queries, candidates, count)
    dense = score(every, table, lengths, passages)
    return give_back(dense, candidates, count)


def solution(mesh):
    in_specs = (
        P(("group", "shard"), None, None),
        P("shard", None, None),
        P("shard"),
        P(("group", "shard"), None),
    )
    out_specs = P(("group", "shard"), None)
    return jax.shard_map(shards, mesh=mesh, in_specs=in_specs, out_specs=out_specs, check_vma=False)
```

time: 905 us -> 71.9 us (0.08)
  local copies, waits for them, and re-layouts: 570 us -> 12.7 us
  matrix products: 183 us -> 0 us
  waiting for transfers between devices: 83.6 us -> 0 us
  Pallas kernels: 0 us -> 59 us
  blocking collectives: 26.4 us -> 0 us
  other arithmetic: 19.6 us -> 0 us
  between operations: 13.5 us -> 0.04 us
    gather x32 -> x0, local copies, waits for them, and re-layouts: 534 us -> none  [score_block(): jnp.take(passage_flat, flat_pass, axis=0).reshape(-1, plen_local, dim_local)]
    dot_general x34 -> x0, matrix products: 183 us -> none  [the longest x16 147 us: score_block(): jnp.einsum('bid,btd->bit', query_block, passage_block, preferred_element_...]
    reduce_scatter x1 -> x0, waiting for transfers between devices: 82.8 us -> none  [shards(): lax.psum_scatter(dense_rows.reshape(shard_count * query_count, cand_count...]
    pallas_call x0 -> x3, Pallas kernels: none -> 59 us  [the longest x1 27.2 us: gather(): pl.pallas_call(functools.partial(gather_kernel, count), out_shape=(jax.Sh...]
    all_gather x1 -> x0, blocking collectives: 26.4 us -> none  [shards(): all_lists = lax.all_gather(candidates, 'shard', axis=0, tiled=True)]
    reshape x38 -> x0, local copies, waits for them, and re-layouts: 11.1 us -> none  [the longest x1 7.35 us: shards(): all_queries.reshape(rounds, merged, query_count, qtok_local * dim_local)]
    another operation x3 -> x0, other arithmetic: 9.14 us -> none
  transfers between devices with their start and end apart: 2 -> 0, of which waited for: 1 -> 0; matrix products, arithmetic and copies ran while one was open for 4% -> 0% of each run, Pallas kernels for 0% -> 0%
where the time goes in v1:
time: 71.9 us; the launch traced here: 71.7 us
  Pallas kernels  59 us (82%)
  local copies, waits for them, and re-layouts  12.7 us (18%)
    pallas_call x1, Pallas kernels, gather(): pl.pallas_call(functools.partial(gather_kernel, count), out_shape=(jax.Sh...  27.2 us
    pallas_call x1, Pallas kernels, give_back(): pl.pallas_call(functools.partial(return_kernel, count), out_shape=jax.Sha...  19.8 us
    unnamed x10, local copies, waits for them, and re-layouts  12.7 us
    pallas_call x1, Pallas kernels, score(): pl.pallas_call(score_kernel, out_shape=jax.ShapeDtypeStruct((qcount, pcou...  12 us

profile of v1, /device:TPU:1, one launch (start us, length us, event | category | flops | bytes accessed | tf_op | source)
XLA Modules:
  0.0 71.7 jit_solution(15308977350461978443)
XLA Ops:
  0.0 0.0 copy-start.1
  0.0 0.9 %copy-done.1 = bf16[16,32,128]{2,1,0:T(8,128)(2,1)S(1)} copy-done((bf16[16,32,128]{2,1,0:T(8,128)(2,1)S(1)}, bf16[16,32,128]{2,1,0:T(8,128)(2,1)}, u32[]{:S(2)}) %copy-start.1) | copy-done | bytes 131096
  0.9 0.0 copy-start.2
  0.9 0.7 copy-done.2
  1.6 27.2 %gather.1 = (bf16[512,32,128]{2,1,0:T(8,128)(2,1)S(1)}, bf16[512,128]{1,0:T(8,128)(2,1)S(1)}) custom-call(bf16[16,32,128]{2,1,0:T(8,128)(2,1)S(1)} %copy-done.1, s32[16,64]{1,0:T(8,128)S(1)} %copy-done.2), custom_call_target="tpu_custom_call" | custom-call | tf_op jit(solution)/shard_map/gather/pallas_call | solution.py:269
  28.8 0.0 copy-start.3
  28.8 9.1 %copy.5.passages = bf16[128,180,128]{2,1,0:T(8,128)(2,1)} copy(bf16[128,180,128]{2,0,1:T(8,128)(2,1)} %param.5) | data formatting | bytes 11796480 | tf_op args[1]
  37.9 0.0 copy-done.3
  37.9 12.0 %score.1.dense = f32[512,128]{1,0:T(8,128)S(1)} custom-call(s32[128]{0:T(128)S(1)} %copy-done.3, bf16[512,32,128]{2,1,0:T(8,128)(2,1)S(1)} %get-tuple-element.7.qall, bf16[512,128]{1,0:T(8,128)(2,1)S(1)} %get-tuple-element.8.table, s32[1,128]{1,0:T(1,128)S(1)} %bitcast.1, bf16[128,180,128]{2,1,0:T(8,128)(2,1)} %copy.5.passages), custom_call_target="tpu_custom_call" | custom-call | tf_op jit(solution)/shard_map/score/pallas_call | solution.py:108
  49.9 0.0 copy-start
  49.9 0.7 copy-done
  50.6 19.8 %give_back.1 = f32[16,64]{1,0:T(8,128)} custom-call(f32[512,128]{1,0:T(8,128)} %copy-done, s32[16,64]{1,0:T(8,128)} %cand_ref.3), custom_call_target="tpu_custom_call" | custom-call | tf_op jit(solution)/shard_map/give_back/pallas_call | solution.py:334
  70.4 1.3 %copy.7 = f32[16,64]{1,0:T(8,128)} copy(f32[16,64]{1,0:T(8,128)} %give_back.1) | data formatting | bytes 8192
Async XLA Ops:
  0.0 0.9 %copy-start.1 = (bf16[16,32,128]{2,1,0:T(8,128)(2,1)S(1)}, bf16[16,32,128]{2,1,0:T(8,128)(2,1)}, u32[]{:S(2)}) copy-start(bf16[16,32,128]{2,1,0:T(8,128)(2,1)} %q_ref.1) | copy-start | bytes 393220
  0.9 0.7 copy-start.2
  28.8 9.1 %copy-start.3 = (s32[128]{0:T(128)S(1)}, s32[128]{0:T(128)}, u32[]{:S(2)}) copy-start(s32[128]{0:T(128)} %len_smem.1) | copy-start | bytes 1540
  49.9 0.7 copy-start

commit v2 on v1

v2 whole, which is shorter than its diff:
```python
import functools

import jax
import jax.numpy as jnp
from jax import lax
from jax.experimental import pallas as pl
from jax.experimental.pallas import tpu as pltpu
from jax.sharding import PartitionSpec as P

F32, BF16, I32 = jnp.float32, jnp.bfloat16, jnp.int32
MESH = pl.DeviceIdType.MESH
SIDE = 4
LANES = 128
UNROLL = 16
BOUNDS = (48, 96, 144)


def nt(a, b):
    return lax.dot_general(a, b, (((1,), (1,)), ((), ())), preferred_element_type=F32)


def place_of(cand, pass_dev):
    half = pass_dev // 2
    within = cand % pass_dev
    owner = cand // (2 * pass_dev) * 2 + within // half
    return owner, cand // pass_dev % 2 * half + within % half


def meet(me, count):
    barrier = pltpu.get_barrier_semaphore()

    def tell(k, _):
        pl.semaphore_signal(barrier, inc=1, device_id={"shard": (me + k) % count}, device_id_type=MESH)
        return 0

    lax.fori_loop(1, count, tell, 0)
    return lambda: pl.semaphore_wait(barrier, count - 1)


def gather_kernel(
    count,
    q_ref,
    cand_ref,
    pass_ref,
    len_ref,
    qall,
    pbuf,
    lists,
    ranks,
    owners,
    cand_buf,
    lens_near,
    lens_far,
    wide,
    slabs,
    table,
    stage,
    send,
    recv,
    near_send,
    near_recv,
    slab_send,
    slab_recv,
    own_sem,
    pass_send,
    pass_recv,
):
    me = lax.axis_index("shard")
    core, x, y = me % 2, (me // 2) % SIDE, me // (2 * SIDE)
    block, ids = cand_ref.shape
    plen, pcount, dim = pass_ref.shape
    qcount = qall.shape[0]
    tiles = ranks.shape[0]
    slots = tiles * LANES
    part, phalf = block // 2, pcount // 2
    sibling = me + 1 - 2 * core
    arrive = meet(me, count)
    own_half = pl.ds(pl.multiple_of(core * phalf, phalf), phalf)
    other_half = pl.ds(pl.multiple_of((1 - core) * phalf, phalf), phalf)
    fetch_cand = pltpu.make_async_copy(cand_ref, cand_buf, own_sem.at[0])
    fetch_pass = pltpu.make_async_copy(pass_ref.at[:, own_half, :], stage.at[:, own_half, :], own_sem.at[1])
    fetch_q = pltpu.make_async_copy(q_ref, qall.at[pl.ds(me * block, block)], own_sem.at[2])
    fetch_len = pltpu.make_async_copy(len_ref, lens_near, own_sem.at[3])
    for fetch in (fetch_cand, fetch_pass, fetch_q, fetch_len):
        fetch.start()

    fetch_cand.wait()
    owner, local = place_of(cand_buf[...], pcount)
    across = lax.broadcasted_iota(I32, (ids, pcount), 1)
    down = lax.broadcasted_iota(I32, (count, ids), 0)
    local_down = jnp.transpose(local.astype(F32)).astype(I32)
    for q in range(block):
        by_owner = jnp.where(owner[q : q + 1] == down, 1.0, 0.0).astype(BF16)
        by_local = jnp.where(local_down[:, q : q + 1] == across, 1.0, 0.0).astype(BF16)
        wide[:, q, :] = jnp.dot(by_owner, by_local, preferred_element_type=F32)
    slabs[...] = wide[...].astype(BF16)
    arrive()

    def device(half, first, second):
        px, py = (first, second) if half == 0 else (second, first)
        return ((py + SIDE) % SIDE * SIDE + (px + SIDE) % SIDE) * 2 + core

    pos = ((x, y), (y, x))
    waits = []

    def push(half, index, first, second, piece, target, own=False):
        a, b = pos[half]
        offset = half * part + piece[0]
        start = device(half, a + first, b + second) * block + offset
        dst = qall.at[pl.ds(start, piece[1])]
        near = target is None
        copy = pltpu.make_async_remote_copy(
            src_ref=q_ref.at[pl.ds(offset, piece[1])] if own else dst,
            dst_ref=dst,
            send_sem=(near_send if near else send).at[half, index],
            recv_sem=(near_recv if near else recv).at[half, index],
            device_id={"shard": sibling if near else device(half, a + target[0], b + target[1])},
            device_id_type=MESH,
        )
        copy.start()
        waits.append(copy.wait_send)
        if near:
            waits.append(copy.wait_recv)
        return copy

    def slab_copy(k):
        peer = (me + k) % count
        return pltpu.make_async_remote_copy(
            src_ref=slabs.at[peer],
            dst_ref=table.at[pl.ds(pl.multiple_of(me * block, block), block)],
            send_sem=slab_send.at[k],
            recv_sem=slab_recv.at[k],
            device_id={"shard": peer},
            device_id_type=MESH,
        )

    def each(action):
        def go(k, _):
            action(slab_copy(k))
            return 0

        lax.fori_loop(1, count, go, 0)

    full, low, high = (0, part), (0, part // 2), (part // 2, part // 2)
    halves = (0, 1)
    a = [push(h, 0, 0, 0, full, (1, 0), True) for h in halves]
    b = [push(h, 1, 0, 0, full, (-1, 0), True) for h in halves]
    up, down_ = {}, {}

    def second_axis(h, j, offset):
        up[h, j] = push(h, 4 + 4 * j, offset, 0, full, (0, 1), j == 0)
        down_[h, j] = push(h, 5 + 4 * j, offset, 0, full, (0, -1), j == 0)

    for h in halves:
        second_axis(h, 0, 0)
    each(lambda copy: copy.start())

    def to_sibling(src, dst, index):
        copy = pltpu.make_async_remote_copy(
            src_ref=src,
            dst_ref=dst,
            send_sem=pass_send.at[index],
            recv_sem=pass_recv.at[index],
            device_id={"shard": sibling},
            device_id_type=MESH,
        )
        copy.start()
        return copy

    give_pass = to_sibling(pass_ref.at[:, other_half, :], stage.at[:, own_half, :], 0)
    give_len = to_sibling(len_ref, lens_far, 1)
    for h in halves:
        push(h, 0, 0, 0, full, None, True)
    table[pl.ds(pl.multiple_of(me * block, block), block), :] = slabs[me]

    def relay(which):
        first = which * phalf

        def go(i, _):
            p = pl.multiple_of(first + i % (phalf // 16) * 16, 16)
            t = pl.multiple_of(i // (phalf // 16) * 16, 16)
            pbuf[pl.ds(p, 16), pl.ds(t, 16), :] = jnp.swapaxes(stage[pl.ds(t, 16), pl.ds(p, 16), :], 0, 1)
            return 0

        lax.fori_loop(0, plen // 16 * (phalf // 16), go, 0)
        rest = plen // 16 * 16
        if rest < plen:
            for i in range(phalf // 16):
                p = pl.multiple_of(first + i * 16, 16)
                pbuf[pl.ds(p, 16), rest:plen, :] = jnp.swapaxes(stage[rest:plen, pl.ds(p, 16), :], 0, 1)

    fetch_pass.wait()
    relay(core)

    shift = (0, -1, 1, 2)
    last = []

    def second_forward(j):
        for h in halves:
            up[h, j].wait_recv()
            last.append(push(h, 6 + 4 * j, shift[j], -1, low, (0, 1)))
            down_[h, j].wait_recv()
            last.append(push(h, 7 + 4 * j, shift[j], 1, high, (0, -1)))

    def second_near(j):
        for h in halves:
            push(h, 4 + 4 * j, shift[j], -1, full, None)
            push(h, 5 + 4 * j, shift[j], 1, full, None)

    c, d = [], []
    for h in halves:
        a[h].wait_recv()
        c.append(push(h, 2, -1, 0, low, (1, 0)))
        second_axis(h, 1, -1)
        b[h].wait_recv()
        d.append(push(h, 3, 1, 0, high, (-1, 0)))
        second_axis(h, 2, 1)
    second_forward(0)
    for h in halves:
        push(h, 1, -1, 0, full, None)
        push(h, 2, 1, 0, full, None)
    second_near(0)

    each(lambda copy: copy.wait_recv())
    hit = table[...]
    row = lax.broadcasted_iota(I32, (qcount, qcount), 0)
    col = lax.broadcasted_iota(I32, (qcount, qcount), 1)
    rank = jnp.dot(jnp.where(col < row, 1.0, 0.0).astype(BF16), hit, preferred_element_type=F32)
    number = lax.dot_general(hit, jnp.ones((qcount, pcount), BF16), (((0,), (0,)), ((), ())), preferred_element_type=F32)
    blocks = jnp.floor((number + 7.0) * 0.125)
    fetch_len.wait()
    give_len.wait_recv()
    mine, theirs = lens_near[...].astype(F32), lens_far[...].astype(F32)
    even, odd = jnp.where(core == 0, mine, theirs), jnp.where(core == 0, theirs, mine)
    lens = jnp.where(
        core == 0,
        jnp.concatenate([even[:, :phalf], odd[:, :phalf]], axis=1),
        jnp.concatenate([even[:, phalf:], odd[:, phalf:]], axis=1),
    )

    def class_of(lens):
        return sum(jnp.where(lens > float(bound), 1.0, 0.0) for bound in BOUNDS)

    lens_down = jnp.transpose(jnp.broadcast_to(lens, (pcount, pcount)))
    class_down = class_of(lens_down)
    p_down = lax.broadcasted_iota(I32, (pcount, LANES), 0).astype(F32)
    lane = lax.broadcasted_iota(I32, (pcount, LANES), 1).astype(F32)
    ahead = jnp.where(class_of(lens) * pcount + lane < class_down * pcount + p_down, 1.0, 0.0).astype(BF16)
    base = jnp.dot(ahead, blocks.astype(BF16), preferred_element_type=F32)
    block_of = jnp.floor(rank * 0.125)
    keyed = jnp.concatenate(
        [jnp.where(hit > 0, block_of, 128.0).astype(BF16), (rank - 8.0 * block_of).astype(BF16)], axis=1
    )
    q_down = lax.broadcasted_iota(I32, (qcount, LANES), 0).astype(F32)
    ends = [
        jnp.sum(jnp.where(class_down <= float(i), blocks, 0.0), axis=0, keepdims=True).astype(I32)
        for i in range(len(BOUNDS) + 1)
    ]

    def list_tile(j):
        slot = lane + float(j * LANES)
        owner = jnp.where(jnp.logical_and(slot >= base, slot < base + blocks), 1.0, 0.0)
        passage = jnp.sum(owner * p_down, axis=0, keepdims=True)
        first = jnp.sum(owner * base, axis=0, keepdims=True)
        length = jnp.sum(owner * lens_down, axis=0, keepdims=True)
        owners[j] = owner.astype(BF16)
        weights = jnp.concatenate([(owner * 8.0).astype(BF16), owner.astype(BF16)], axis=0)
        seen = jnp.dot(keyed, weights, preferred_element_type=F32) - 8.0 * (slot[:1] - first)
        ranks[j] = seen
        rows = [jnp.sum(jnp.where(seen == float(k), q_down, 0.0), axis=0, keepdims=True) for k in range(8)]
        rows = [jnp.clip(r.astype(I32), 0, qcount - 1) for r in rows]
        rows += [jnp.clip(passage.astype(I32), 0, pcount - 1)] + ends + [length.astype(I32)]
        for k, r in enumerate(rows):
            lists[k : k + 1, j * LANES : (j + 1) * LANES] = r

    for h in halves:
        c[h].wait_recv()
        d[h].wait_recv()
        second_axis(h, 3, 2)
    for h in halves:
        push(h, 3, 2, 0, full, None)
    for j in range(tiles // 2):
        list_tile(j)
    for j in (1, 2):
        second_forward(j)
    for j in (1, 2):
        second_near(j)
    for j in range(tiles // 2, tiles):
        list_tile(j)
    second_forward(3)
    second_near(3)
    give_pass.wait_recv()
    relay(1 - core)
    for i, (j, h) in enumerate((j, h) for j in range(4) for h in halves):
        last[2 * i].wait_recv()
        last[2 * i + 1].wait_recv()
        push(h, 6 + 4 * j, shift[j], 2, full, None)
    for wait in waits:
        wait()
    each(lambda copy: copy.wait_send())
    give_pass.wait_send()
    give_len.wait_send()
    fetch_q.wait()


def gather(queries, candidates, passages, lengths, count):
    block, qtok, dim = queries.shape
    plen, pcount, _ = passages.shape
    most = (2 * 3 * candidates.size + 7 * pcount) // 8
    tiles = -(-(most + UNROLL - 1) // LANES)
    vmem, hbm = pl.BlockSpec(memory_space=pltpu.VMEM), pl.BlockSpec(memory_space=pl.ANY)
    dma = pltpu.SemaphoreType.DMA
    args = [pltpu.with_memory_space_constraint(v, pltpu.HBM) for v in (queries, candidates, passages, lengths)]
    return pl.pallas_call(
        functools.partial(gather_kernel, count),
        out_shape=(
            jax.ShapeDtypeStruct((count * block, qtok, dim), BF16),
            jax.ShapeDtypeStruct((pcount, plen, dim), BF16),
            jax.ShapeDtypeStruct((16, tiles * LANES), I32),
            jax.ShapeDtypeStruct((tiles, count * block, LANES), F32),
            jax.ShapeDtypeStruct((tiles, pcount, LANES), BF16),
        ),
        in_specs=[hbm] * 4,
        out_specs=(vmem,) * 5,
        scratch_shapes=[
            pltpu.VMEM(candidates.shape, I32),
            pltpu.VMEM((1, pcount), I32),
            pltpu.VMEM((1, pcount), I32),
            pltpu.VMEM((count, block, pcount), F32),
            pltpu.VMEM((count, block, pcount), BF16),
            pltpu.VMEM((count * block, pcount), BF16),
            pltpu.VMEM((plen, pcount, dim), BF16),
            dma((2, 20)),
            dma((2, 20)),
            dma((2, 20)),
            dma((2, 20)),
            dma((count,)),
            dma((count,)),
            dma((4,)),
            dma((2,)),
            dma((2,)),
        ],
        compiler_params=pltpu.CompilerParams(collective_id=0, has_side_effects=True, vmem_limit_bytes=28 << 20),
        name="gather",
    )(*args)


def score_kernel(qall, pbuf, lists, ranks, owners, out, acc, table, sem):
    qcount, qtok, dim = qall.shape
    pcount, plen, _ = pbuf.shape
    move = pltpu.make_async_copy(lists, table, sem)
    move.start()
    move.wait()
    start = 0
    for c, rows in enumerate(BOUNDS + (plen,)):
        end = table[9 + c, 0]
        down = lax.broadcasted_iota(I32, (rows, 1), 0)

        def step(i, _, start=start, rows=rows, down=down):
            for u in range(UNROLL):
                b = start + i * UNROLL + u
                tokens = jnp.concatenate([qall[table[k, b]] for k in range(8)], axis=0)
                similar = nt(pbuf[table[8, b], :rows], tokens)
                similar = jnp.where(down < table[13, b], similar, -1e30)
                acc[pl.ds(b, 1), :] = jnp.max(similar, axis=0, keepdims=True)
            return 0

        lax.fori_loop(0, (end - start + UNROLL - 1) // UNROLL, step, 0)
        start = end
    token = lax.broadcasted_iota(I32, (8, 8 * qtok), 1)
    mean = jnp.where(token // qtok == lax.broadcasted_iota(I32, (8, 8 * qtok), 0), 1.0 / qtok, 0.0).astype(BF16)
    out[...] = jnp.zeros_like(out)

    def spread(j, _):
        best = acc[pl.ds(pl.multiple_of(j * LANES, LANES), LANES), :]
        high = best.astype(BF16)
        scores = nt(mean, high) + nt(mean, (best - high.astype(F32)).astype(BF16))
        seen = ranks[j]
        dense = sum(jnp.where(seen == float(k), scores[k : k + 1], 0.0) for k in range(8))
        high = dense.astype(BF16)
        both = jnp.concatenate([high, (dense - high.astype(F32)).astype(BF16)], axis=1)
        out[...] += nt(both, jnp.concatenate([owners[j]] * 2, axis=1))
        return 0

    lax.fori_loop(0, (start + LANES - 1) // LANES, spread, 0)


def score(every, passages, lists, ranks, owners):
    qcount, qtok, _ = every.shape
    pcount = passages.shape[0]
    slots = lists.shape[1]
    vmem = pl.BlockSpec(memory_space=pltpu.VMEM)
    return pl.pallas_call(
        score_kernel,
        out_shape=jax.ShapeDtypeStruct((qcount, pcount), F32),
        in_specs=[vmem] * 5,
        out_specs=vmem,
        scratch_shapes=[
            pltpu.VMEM((slots, 8 * qtok), F32),
            pltpu.SMEM((16, slots), I32),
            pltpu.SemaphoreType.DMA,
        ],
        compiler_params=pltpu.CompilerParams(vmem_limit_bytes=20 << 20),
        name="score",
    )(every, passages, lists, ranks, owners)


def return_kernel(count, pcount, dense, cand_ref, out, slabs, send, recv):
    me = lax.axis_index("shard")
    block, ids = cand_ref.shape
    meet(me, count)()

    def slab_copy(k):
        peer = (me + k) % count
        return pltpu.make_async_remote_copy(
            src_ref=dense.at[pl.ds(pl.multiple_of(peer * block, block), block)],
            dst_ref=slabs.at[me],
            send_sem=send.at[k],
            recv_sem=recv.at[k],
            device_id={"shard": peer},
            device_id_type=MESH,
        )

    def each(action):
        def go(k, _):
            action(slab_copy(k))
            return 0

        lax.fori_loop(1, count, go, 0)

    each(lambda copy: copy.start())
    slabs[me] = dense[pl.ds(pl.multiple_of(me * block, block), block), :]
    owner, local = place_of(cand_ref[...], pcount)
    local = jnp.concatenate([local] * (pcount // ids), axis=1)
    each(lambda copy: copy.wait())
    total = jnp.zeros((block, ids), F32)
    for o in range(count):
        found = jnp.take_along_axis(slabs[o], local, axis=1)[:, :ids]
        total = jnp.where(owner == o, found, total)
    out[...] = total


def give_back(dense, candidates, count):
    block, ids = candidates.shape
    pcount = dense.shape[1]
    vmem = pl.BlockSpec(memory_space=pltpu.VMEM)
    dma = pltpu.SemaphoreType.DMA
    return pl.pallas_call(
        functools.partial(return_kernel, count, pcount),
        out_shape=jax.ShapeDtypeStruct((block, ids), F32),
        in_specs=[vmem, vmem],
        out_specs=vmem,
        scratch_shapes=[pltpu.VMEM((count, block, pcount), F32), dma((count,)), dma((count,))],
        compiler_params=pltpu.CompilerParams(collective_id=1, has_side_effects=True, vmem_limit_bytes=8 << 20),
        name="give_back",
    )(dense, candidates)


def shards(queries, passages, lengths, candidates):
    count = lax.axis_size("shard")
    tokens_first = jnp.swapaxes(passages, 0, 1)
    every, kept, lists, ranks, owners = gather(queries, candidates, tokens_first, lengths.reshape(1, -1), count)
    return give_back(score(every, kept, lists, ranks, owners), candidates, count)


def solution(mesh):
    in_specs = (
        P(("group", "shard"), None, None),
        P("shard", None, None),
        P("shard"),
        P(("group", "shard"), None),
    )
    out_specs = P(("group", "shard"), None)
    return jax.shard_map(shards, mesh=mesh, in_specs=in_specs, out_specs=out_specs, check_vma=False)
```

time: 71.9 us -> 51.7 us (0.72)
  local copies, waits for them, and re-layouts: 12.7 us -> 0.61 us
  Pallas kernels: 59 us -> 51 us
    unnamed x10 -> x3, local copies, waits for them, and re-layouts: 12.7 us -> 0.61 us
    pallas_call x1, Pallas kernels: 19.8 us -> 14.2 us  [give_back(): pl.pallas_call(functools.partial(return_kernel, count, pcount), out_shape...]
    pallas_call x1, Pallas kernels: 12 us -> 9.53 us  [score(): pl.pallas_call(score_kernel, out_shape=jax.ShapeDtypeStruct((qcount, pcou...]
where the time goes in v2:
time: 51.7 us; the launch traced here: 51.6 us
  Pallas kernels  51 us (99%)
  local copies, waits for them, and re-layouts  0.61 us (1%)
    pallas_call x1, Pallas kernels, gather(): pl.pallas_call(functools.partial(gather_kernel, count), out_shape=(jax.Sh...  27.3 us
    pallas_call x1, Pallas kernels, give_back(): pl.pallas_call(functools.partial(return_kernel, count, pcount), out_shape...  14.2 us
    pallas_call x1, Pallas kernels, score(): pl.pallas_call(score_kernel, out_shape=jax.ShapeDtypeStruct((qcount, pcou...  9.53 us

profile of v2, /device:TPU:1, one launch (start us, length us, event | category | flops | bytes accessed | tf_op | source)
XLA Modules:
  0.0 51.6 jit_solution(9165411513503103404)
XLA Ops:
  0.0 27.3 %gather.1 = (bf16[512,32,128]{2,1,0:T(8,128)(2,1)S(1)}, bf16[128,180,128]{2,1,0:T(8,128)(2,1)S(1)}, s32[16,896]{1,0:T(8,128)S(1)}, f32[7,512,128]{2,1,0:T(8,128)S(1)}, bf16[7,128,128]{2,1,0:T(8,128)(2,1)S(1)}) custom-call(bf16[16,32,128]{2,1,0:T(8,128)(2,1)} %q_ref.1, s32[16,64]{1,0:T(8,128)} %cand_ref.3, bf16[180,128,128]{2,1,0:T(8,128)(2,1)} %bitcast.2, ...), custom_call_target="tpu_custom_call" | custom-call | tf_op jit(solution)/shard_map/gather/pallas_call | solution.py:314
  27.3 0.0 copy-start
  27.3 9.5 %score.1.dense = f32[512,128]{1,0:T(8,128)S(1)} custom-call(bf16[512,32,128]{2,1,0:T(8,128)(2,1)S(1)} %get-tuple-element.10.qall, bf16[128,180,128]{2,1,0:T(8,128)(2,1)S(1)} %get-tuple-element.11.pbuf, s32[16,896]{1,0:T(8,128)S(1)} %get-tuple-element.12.lists, f32[7,512,128]{2,1,0:T(8,128)S(1)} %get-tuple-element.13.ranks, ...), custom_call_target="tpu_custom_call" | custom-call | tf_op jit(solution)/shard_map/score/pallas_call | solution.py:393
  36.8 0.0 copy-done
  36.8 14.2 %give_back.1 = f32[16,64]{1,0:T(8,128)S(1)} custom-call(f32[512,128]{1,0:T(8,128)S(1)} %score.1.dense, s32[16,64]{1,0:T(8,128)S(1)} %copy-done), custom_call_target="tpu_custom_call" | custom-call | tf_op jit(solution)/shard_map/give_back/pallas_call | solution.py:448
  51.0 0.6 %copy.6 = f32[16,64]{1,0:T(8,128)} copy(f32[16,64]{1,0:T(8,128)S(1)} %give_back.1) | data formatting | bytes 8192
Async XLA Ops:
  27.3 9.5 %copy-start = (s32[16,64]{1,0:T(8,128)S(1)}, s32[16,64]{1,0:T(8,128)}, u32[]{:S(2)}) copy-start(s32[16,64]{1,0:T(8,128)} %cand_ref.3) | copy-start | bytes 12292

commit v3 on v2

--- a/solution.py
+++ b/solution.py
@@ -12,6 +12,7 @@
 SIDE = 4
 LANES = 128
 UNROLL = 16
+ROOM = 256
 BOUNDS = (48, 96, 144)
 
 
@@ -48,12 +49,17 @@
     lists,
     ranks,
     owners,
+    pairs_q,
+    pairs_p,
+    spots,
     cand_buf,
     lens_near,
     lens_far,
-    wide,
     slabs,
     table,
+    codes_q,
+    codes_p,
+    hits,
     stage,
     send,
     recv,
@@ -84,16 +90,6 @@
     for fetch in (fetch_cand, fetch_pass, fetch_q, fetch_len):
         fetch.start()
 
-    fetch_cand.wait()
-    owner, local = place_of(cand_buf[...], pcount)
-    across = lax.broadcasted_iota(I32, (ids, pcount), 1)
-    down = lax.broadcasted_iota(I32, (count, ids), 0)
-    local_down = jnp.transpose(local.astype(F32)).astype(I32)
-    for q in range(block):
-        by_owner = jnp.where(owner[q : q + 1] == down, 1.0, 0.0).astype(BF16)
-        by_local = jnp.where(local_down[:, q : q + 1] == across, 1.0, 0.0).astype(BF16)
-        wide[:, q, :] = jnp.dot(by_owner, by_local, preferred_element_type=F32)
-    slabs[...] = wide[...].astype(BF16)
     arrive()
 
     def device(half, first, second):
@@ -127,7 +123,7 @@
         peer = (me + k) % count
         return pltpu.make_async_remote_copy(
             src_ref=slabs.at[peer],
-            dst_ref=table.at[pl.ds(pl.multiple_of(me * block, block), block)],
+            dst_ref=table.at[me],
             send_sem=slab_send.at[k],
             recv_sem=slab_recv.at[k],
             device_id={"shard": peer},
@@ -153,7 +149,7 @@
 
     for h in halves:
         second_axis(h, 0, 0)
-    each(lambda copy: copy.start())
+    c = [push(h, 2, 0, 0, full, (2, 0), True) for h in halves]
 
     def to_sibling(src, dst, index):
         copy = pltpu.make_async_remote_copy(
@@ -171,7 +167,34 @@
     give_len = to_sibling(len_ref, lens_far, 1)
     for h in halves:
         push(h, 0, 0, 0, full, None, True)
-    table[pl.ds(pl.multiple_of(me * block, block), block), :] = slabs[me]
+
+    fetch_cand.wait()
+    owner, local = place_of(cand_buf[...], pcount)
+    local = local.astype(F32)
+    down = lax.broadcasted_iota(I32, (count, ids), 0)
+    by_owner = [jnp.where(owner[q : q + 1] == down, 1.0, 0.0) for q in range(block)]
+    stack = jnp.concatenate(by_owner, axis=0).astype(BF16)
+    earlier = lax.broadcasted_iota(I32, (ids, ids), 0) < lax.broadcasted_iota(I32, (ids, ids), 1)
+    prior = jnp.dot(stack, jnp.where(earlier, 1.0, 0.0).astype(BF16), preferred_element_type=F32)
+    totals = jnp.dot(stack, jnp.ones((ids, ids), BF16), preferred_element_type=F32)
+    running = jnp.zeros((count, ids), F32)
+    spot = []
+    for q in range(block):
+        spot.append(jnp.sum(by_owner[q] * (prior[q * count : (q + 1) * count] + running), axis=0, keepdims=True))
+        running = running + totals[q * count : (q + 1) * count]
+    spot = jnp.concatenate(spot, axis=0)
+    spots[...] = spot.astype(I32)
+    spot_down = jnp.transpose(spot).astype(I32)
+    across = lax.broadcasted_iota(I32, (ids, ROOM), 1)
+    code = jnp.zeros((count, ROOM), F32)
+    for q in range(block):
+        values = jnp.concatenate([by_owner[q] * local[q : q + 1], by_owner[q]], axis=0).astype(BF16)
+        put = jnp.where(spot_down[:, q : q + 1] == across, 1.0, 0.0).astype(BF16)
+        found = jnp.dot(values, put, preferred_element_type=F32)
+        code = code + found[:count] + found[count:] * float(pcount * (q + 1))
+    slabs[:, 0, :] = code
+    each(lambda copy: copy.start())
+    table[me] = slabs[me]
 
     def relay(which):
         first = which * phalf
@@ -207,22 +230,39 @@
             push(h, 4 + 4 * j, shift[j], -1, full, None)
             push(h, 5 + 4 * j, shift[j], 1, full, None)
 
-    c, d = [], []
     for h in halves:
         a[h].wait_recv()
-        c.append(push(h, 2, -1, 0, low, (1, 0)))
         second_axis(h, 1, -1)
         b[h].wait_recv()
-        d.append(push(h, 3, 1, 0, high, (-1, 0)))
         second_axis(h, 2, 1)
     second_forward(0)
     for h in halves:
+        c[h].wait_recv()
+        second_axis(h, 3, 2)
+    for h in halves:
         push(h, 1, -1, 0, full, None)
         push(h, 2, 1, 0, full, None)
+        push(h, 3, 2, 0, full, None)
     second_near(0)
 
     each(lambda copy: copy.wait_recv())
-    hit = table[...]
+    codes = table[:, 0, :]
+    which_q = jnp.floor(codes * (1.0 / pcount))
+    codes_q[...] = which_q - 1.0
+    codes_p[...] = codes - which_q * pcount
+
+    def unpack(i, _):
+        q_iota = lax.broadcasted_iota(I32, (block, ROOM), 0).astype(F32)
+        p_iota = lax.broadcasted_iota(I32, (pcount, ROOM), 0).astype(F32)
+        is_q = jnp.where(codes_q[pl.ds(i, 1), :] == q_iota, 1.0, 0.0).astype(BF16)
+        is_p = jnp.where(codes_p[pl.ds(i, 1), :] == p_iota, 1.0, 0.0).astype(BF16)
+        pairs_q[i] = is_q
+        pairs_p[i] = is_p
+        hits[pl.ds(pl.multiple_of(i * block, block), block), :] = nt(is_q, is_p).astype(BF16)
+        return 0
+
+    lax.fori_loop(0, count, unpack, 0, unroll=8)
+    hit = hits[...]
     row = lax.broadcasted_iota(I32, (qcount, qcount), 0)
     col = lax.broadcasted_iota(I32, (qcount, qcount), 1)
     rank = jnp.dot(jnp.where(col < row, 1.0, 0.0).astype(BF16), hit, preferred_element_type=F32)
@@ -273,12 +313,6 @@
         for k, r in enumerate(rows):
             lists[k : k + 1, j * LANES : (j + 1) * LANES] = r
 
-    for h in halves:
-        c[h].wait_recv()
-        d[h].wait_recv()
-        second_axis(h, 3, 2)
-    for h in halves:
-        push(h, 3, 2, 0, full, None)
     for j in range(tiles // 2):
         list_tile(j)
     for j in (1, 2):
@@ -319,15 +353,20 @@
             jax.ShapeDtypeStruct((16, tiles * LANES), I32),
             jax.ShapeDtypeStruct((tiles, count * block, LANES), F32),
             jax.ShapeDtypeStruct((tiles, pcount, LANES), BF16),
+            jax.ShapeDtypeStruct((count, block, ROOM), BF16),
+            jax.ShapeDtypeStruct((count, pcount, ROOM), BF16),
+            jax.ShapeDtypeStruct(candidates.shape, I32),
         ),
         in_specs=[hbm] * 4,
-        out_specs=(vmem,) * 5,
+        out_specs=(vmem,) * 8,
         scratch_shapes=[
             pltpu.VMEM(candidates.shape, I32),
             pltpu.VMEM((1, pcount), I32),
             pltpu.VMEM((1, pcount), I32),
-            pltpu.VMEM((count, block, pcount), F32),
-            pltpu.VMEM((count, block, pcount), BF16),
+            pltpu.VMEM((count, 1, ROOM), F32),
+            pltpu.VMEM((count, 1, ROOM), F32),
+            pltpu.VMEM((count, ROOM), F32),
+            pltpu.VMEM((count, ROOM), F32),
             pltpu.VMEM((count * block, pcount), BF16),
             pltpu.VMEM((plen, pcount, dim), BF16),
             dma((2, 20)),
@@ -345,7 +384,7 @@
     )(*args)
 
 
-def score_kernel(qall, pbuf, lists, ranks, owners, out, acc, table, sem):
+def score_kernel(qall, pbuf, lists, ranks, owners, pairs_q, pairs_p, out, acc, total, table, sem):
     qcount, qtok, dim = qall.shape
     pcount, plen, _ = pbuf.shape
     move = pltpu.make_async_copy(lists, table, sem)
@@ -365,11 +404,12 @@
                 acc[pl.ds(b, 1), :] = jnp.max(similar, axis=0, keepdims=True)
             return 0
 
-        lax.fori_loop(0, (end - start + UNROLL - 1) // UNROLL, step, 0)
-        start = end
+        whole = (end - start + (UNROLL - 1 if rows == plen else 0)) // UNROLL
+        lax.fori_loop(0, whole, step, 0)
+        start = start + whole * UNROLL
     token = lax.broadcasted_iota(I32, (8, 8 * qtok), 1)
     mean = jnp.where(token // qtok == lax.broadcasted_iota(I32, (8, 8 * qtok), 0), 1.0 / qtok, 0.0).astype(BF16)
-    out[...] = jnp.zeros_like(out)
+    total[...] = jnp.zeros_like(total)
 
     def spread(j, _):
         best = acc[pl.ds(pl.multiple_of(j * LANES, LANES), LANES), :]
@@ -379,41 +419,58 @@
         dense = sum(jnp.where(seen == float(k), scores[k : k + 1], 0.0) for k in range(8))
         high = dense.astype(BF16)
         both = jnp.concatenate([high, (dense - high.astype(F32)).astype(BF16)], axis=1)
-        out[...] += nt(both, jnp.concatenate([owners[j]] * 2, axis=1))
+        total[...] += nt(both, jnp.concatenate([owners[j]] * 2, axis=1))
         return 0
 
-    lax.fori_loop(0, (start + LANES - 1) // LANES, spread, 0)
-
-
-def score(every, passages, lists, ranks, owners):
+    lax.fori_loop(0, (table[9 + len(BOUNDS), 0] + LANES - 1) // LANES, spread, 0)
+    count, block, _ = pairs_q.shape
+
+    def pack(i, _):
+        rows = total[pl.ds(pl.multiple_of(i * block, block), block), :]
+        high = rows.astype(BF16)
+        both = jnp.concatenate([high, (rows - high.astype(F32)).astype(BF16)], axis=0)
+        found = jnp.dot(both, pairs_p[i], preferred_element_type=F32)
+        found = (found[:block] + found[block:]) * pairs_q[i].astype(F32)
+        out[i] = jnp.sum(found, axis=0, keepdims=True)
+        return 0
+
+    lax.fori_loop(0, count, pack, 0, unroll=8)
+
+
+def score(every, passages, lists, ranks, owners, pairs_q, pairs_p):
     qcount, qtok, _ = every.shape
     pcount = passages.shape[0]
     slots = lists.shape[1]
     vmem = pl.BlockSpec(memory_space=pltpu.VMEM)
     return pl.pallas_call(
         score_kernel,
-        out_shape=jax.ShapeDtypeStruct((qcount, pcount), F32),
-        in_specs=[vmem] * 5,
+        out_shape=jax.ShapeDtypeStruct((pairs_q.shape[0], 1, ROOM), F32),
+        in_specs=[vmem] * 7,
         out_specs=vmem,
         scratch_shapes=[
             pltpu.VMEM((slots, 8 * qtok), F32),
+            pltpu.VMEM((qcount, pcount), F32),
             pltpu.SMEM((16, slots), I32),
             pltpu.SemaphoreType.DMA,
         ],
         compiler_params=pltpu.CompilerParams(vmem_limit_bytes=20 << 20),
         name="score",
-    )(every, passages, lists, ranks, owners)
-
-
-def return_kernel(count, pcount, dense, cand_ref, out, slabs, send, recv):
+    )(every, passages, lists, ranks, owners, pairs_q, pairs_p)
+
+
+def return_kernel(count, pcount, compact, cand_ref, spots, out, slabs, send, recv):
     me = lax.axis_index("shard")
     block, ids = cand_ref.shape
-    meet(me, count)()
+    arrive = meet(me, count)
+    owner, _ = place_of(cand_ref[...], pcount)
+    spot = spots[...]
+    spot_w = jnp.concatenate([spot % LANES] * (LANES // ids), axis=1)
+    arrive()
 
     def slab_copy(k):
         peer = (me + k) % count
         return pltpu.make_async_remote_copy(
-            src_ref=dense.at[pl.ds(pl.multiple_of(peer * block, block), block)],
+            src_ref=compact.at[peer],
             dst_ref=slabs.at[me],
             send_sem=send.at[k],
             recv_sem=recv.at[k],
@@ -429,38 +486,38 @@
         lax.fori_loop(1, count, go, 0)
 
     each(lambda copy: copy.start())
-    slabs[me] = dense[pl.ds(pl.multiple_of(me * block, block), block), :]
-    owner, local = place_of(cand_ref[...], pcount)
-    local = jnp.concatenate([local] * (pcount // ids), axis=1)
+    slabs[me] = compact[me]
     each(lambda copy: copy.wait())
-    total = jnp.zeros((block, ids), F32)
+    result = jnp.zeros((block, ids), F32)
     for o in range(count):
-        found = jnp.take_along_axis(slabs[o], local, axis=1)[:, :ids]
-        total = jnp.where(owner == o, found, total)
-    out[...] = total
-
-
-def give_back(dense, candidates, count):
+        for part in range(ROOM // LANES):
+            row = jnp.broadcast_to(slabs[o, :, part * LANES : (part + 1) * LANES], (block, LANES))
+            found = jnp.take_along_axis(row, spot_w, axis=1)[:, :ids]
+            result = jnp.where(jnp.logical_and(owner == o, spot // LANES == part), found, result)
+    out[...] = result
+
+
+def give_back(compact, candidates, spots, pcount):
     block, ids = candidates.shape
-    pcount = dense.shape[1]
+    count = compact.shape[0]
     vmem = pl.BlockSpec(memory_space=pltpu.VMEM)
     dma = pltpu.SemaphoreType.DMA
     return pl.pallas_call(
         functools.partial(return_kernel, count, pcount),
         out_shape=jax.ShapeDtypeStruct((block, ids), F32),
-        in_specs=[vmem, vmem],
+        in_specs=[vmem] * 3,
         out_specs=vmem,
-        scratch_shapes=[pltpu.VMEM((count, block, pcount), F32), dma((count,)), dma((count,))],
+        scratch_shapes=[pltpu.VMEM((count, 1, ROOM), F32), dma((count,)), dma((count,))],
         compiler_params=pltpu.CompilerParams(collective_id=1, has_side_effects=True, vmem_limit_bytes=8 << 20),
         name="give_back",
-    )(dense, candidates)
+    )(compact, candidates, spots)
 
 
 def shards(queries, passages, lengths, candidates):
     count = lax.axis_size("shard")
     tokens_first = jnp.swapaxes(passages, 0, 1)
-    every, kept, lists, ranks, owners = gather(queries, candidates, tokens_first, lengths.reshape(1, -1), count)
-    return give_back(score(every, kept, lists, ranks, owners), candidates, count)
+    *made, spots = gather(queries, candidates, tokens_first, lengths.reshape(1, -1), count)
+    return give_back(score(*made), candidates, spots, passages.shape[0])
 
 
 def solution(mesh):

time: 51.7 us -> 49.4 us (0.956)
  Pallas kernels: 51 us -> 48.7 us
    pallas_call x1, Pallas kernels: 14.2 us -> 13 us  [give_back(): pl.pallas_call(functools.partial(return_kernel, count, pcount), out_shape...]
    pallas_call x1, Pallas kernels: 27.3 us -> 26.4 us  [gather(): pl.pallas_call(functools.partial(gather_kernel, count), out_shape=(jax.Sh...]
where the time goes in v3:
time: 49.4 us
  Pallas kernels  48.7 us (99%)
  local copies, waits for them, and re-layouts  0.61 us (1%)
    pallas_call x1, Pallas kernels, gather(): pl.pallas_call(functools.partial(gather_kernel, count), out_shape=(jax.Sh...  26.4 us
    pallas_call x1, Pallas kernels, give_back(): pl.pallas_call(functools.partial(return_kernel, count, pcount), out_shape...  13 us
    pallas_call x1, Pallas kernels, score(): pl.pallas_call(score_kernel, out_shape=jax.ShapeDtypeStruct((pairs_q.shap...  9.32 us

profile of v3, /device:TPU:1, one launch (start us, length us, event | category | flops | bytes accessed | tf_op | source)
XLA Modules:
  0.0 49.4 jit_solution(17693785900603608147)
XLA Ops:
  0.0 26.4 %gather.1 = (bf16[512,32,128]{2,1,0:T(8,128)(2,1)S(1)}, bf16[128,180,128]{2,1,0:T(8,128)(2,1)S(1)}, s32[16,896]{1,0:T(8,128)S(1)}, f32[7,512,128]{2,1,0:T(8,128)...) custom-call(bf16[16,32,128]{2,1,0:T(8,128)(2,1)} %q_ref.1, ...), custom_call_target="tpu_custom_call" | custom-call | tf_op jit(solution)/shard_map/gather/pallas_call | solution.py:348
  26.4 0.0 copy-start
  26.4 9.3 %score.1.compact = f32[32,1,256]{2,1,0:T(1,128)S(1)} custom-call(bf16[512,32,128]{2,1,0:T(8,128)(2,1)S(1)} %get-tuple-element.13.qall, bf16[128,180,128]{2,1,0:T(8,128)(2,1)S(1)} %get-tuple-element.14.pbuf, s32[16,896]{1,0:T(8,128)S(1)} %get-tuple-element.15.lists, f32[7,512,128]{2,1,0:T(8,128)S(1)} %get-tuple-element.16.ranks, ...), custom_call_target="tpu_custom_call" | custom-call | tf_op jit(solution)/shard_map/score/pallas_call | solution.py:445
  35.7 0.0 copy-done
  35.7 13.0 %give_back.1 = f32[16,64]{1,0:T(8,128)S(1)} custom-call(f32[32,1,256]{2,1,0:T(1,128)S(1)} %score.1.compact, s32[16,64]{1,0:T(8,128)S(1)} %copy-done, s32[16,64]{1,0:T(8,128)S(1)} %get-tuple-element.20.spots), custom_call_target="tpu_custom_call" | custom-call | tf_op jit(solution)/shard_map/give_back/pallas_call | solution.py:505
  48.8 0.6 %copy.6 = f32[16,64]{1,0:T(8,128)} copy(f32[16,64]{1,0:T(8,128)S(1)} %give_back.1) | data formatting | bytes 8192
Async XLA Ops:
  26.4 9.3 %copy-start = (s32[16,64]{1,0:T(8,128)S(1)}, s32[16,64]{1,0:T(8,128)}, u32[]{:S(2)}) copy-start(s32[16,64]{1,0:T(8,128)} %cand_ref.3) | copy-start | bytes 12292

commit v4 on v3

--- a/solution.py
+++ b/solution.py
@@ -12,6 +12,7 @@
 SIDE = 4
 LANES = 128
 UNROLL = 16
+EARLY = 3
 ROOM = 256
 BOUNDS = (48, 96, 144)
 
@@ -305,7 +306,9 @@
         length = jnp.sum(owner * lens_down, axis=0, keepdims=True)
         owners[j] = owner.astype(BF16)
         weights = jnp.concatenate([(owner * 8.0).astype(BF16), owner.astype(BF16)], axis=0)
+        used = jnp.sum(owner, axis=0, keepdims=True)
         seen = jnp.dot(keyed, weights, preferred_element_type=F32) - 8.0 * (slot[:1] - first)
+        seen = seen - 16.0 * qcount * (1.0 - used)
         ranks[j] = seen
         rows = [jnp.sum(jnp.where(seen == float(k), q_down, 0.0), axis=0, keepdims=True) for k in range(8)]
         rows = [jnp.clip(r.astype(I32), 0, qcount - 1) for r in rows]
@@ -313,16 +316,16 @@
         for k, r in enumerate(rows):
             lists[k : k + 1, j * LANES : (j + 1) * LANES] = r
 
-    for j in range(tiles // 2):
-        list_tile(j)
     for j in (1, 2):
         second_forward(j)
     for j in (1, 2):
         second_near(j)
-    for j in range(tiles // 2, tiles):
+    for j in range(0, 4):
         list_tile(j)
     second_forward(3)
     second_near(3)
+    for j in range(4, tiles):
+        list_tile(j)
     give_pass.wait_recv()
     relay(1 - core)
     for i, (j, h) in enumerate((j, h) for j in range(4) for h in halves):
@@ -384,7 +387,7 @@
     )(*args)
 
 
-def score_kernel(qall, pbuf, lists, ranks, owners, pairs_q, pairs_p, out, acc, total, table, sem):
+def score_kernel(qall, pbuf, lists, ranks, owners, acc, total, table, sem):
     qcount, qtok, dim = qall.shape
     pcount, plen, _ = pbuf.shape
     move = pltpu.make_async_copy(lists, table, sem)
@@ -407,23 +410,59 @@
         whole = (end - start + (UNROLL - 1 if rows == plen else 0)) // UNROLL
         lax.fori_loop(0, whole, step, 0)
         start = start + whole * UNROLL
+    total[...] = jnp.zeros_like(total)
+
+    def late(j, _):
+        spread(j, acc, ranks, owners, total, qtok)
+        return 0
+
+    lax.fori_loop(EARLY, (table[9 + len(BOUNDS), 0] + LANES - 1) // LANES, late, 0)
+
+
+def spread(j, acc, ranks, owners, total, qtok):
     token = lax.broadcasted_iota(I32, (8, 8 * qtok), 1)
     mean = jnp.where(token // qtok == lax.broadcasted_iota(I32, (8, 8 * qtok), 0), 1.0 / qtok, 0.0).astype(BF16)
-    total[...] = jnp.zeros_like(total)
-
-    def spread(j, _):
-        best = acc[pl.ds(pl.multiple_of(j * LANES, LANES), LANES), :]
-        high = best.astype(BF16)
-        scores = nt(mean, high) + nt(mean, (best - high.astype(F32)).astype(BF16))
-        seen = ranks[j]
-        dense = sum(jnp.where(seen == float(k), scores[k : k + 1], 0.0) for k in range(8))
-        high = dense.astype(BF16)
-        both = jnp.concatenate([high, (dense - high.astype(F32)).astype(BF16)], axis=1)
-        total[...] += nt(both, jnp.concatenate([owners[j]] * 2, axis=1))
-        return 0
-
-    lax.fori_loop(0, (table[9 + len(BOUNDS), 0] + LANES - 1) // LANES, spread, 0)
-    count, block, _ = pairs_q.shape
+    best = acc[pl.ds(pl.multiple_of(j * LANES, LANES), LANES), :]
+    high = best.astype(BF16)
+    scores = nt(mean, high) + nt(mean, (best - high.astype(F32)).astype(BF16))
+    seen = ranks[j]
+    dense = sum(jnp.where(seen == float(k), scores[k : k + 1], 0.0) for k in range(8))
+    high = dense.astype(BF16)
+    both = jnp.concatenate([high, (dense - high.astype(F32)).astype(BF16)], axis=1)
+    total[...] += nt(both, jnp.concatenate([owners[j]] * 2, axis=1))
+
+
+def score(every, passages, lists, ranks, owners):
+    qcount, qtok, _ = every.shape
+    pcount = passages.shape[0]
+    slots = lists.shape[1]
+    vmem = pl.BlockSpec(memory_space=pltpu.VMEM)
+    return pl.pallas_call(
+        score_kernel,
+        out_shape=(
+            jax.ShapeDtypeStruct((slots, 8 * qtok), F32),
+            jax.ShapeDtypeStruct((qcount, pcount), F32),
+        ),
+        in_specs=[vmem] * 5,
+        out_specs=(vmem, vmem),
+        scratch_shapes=[
+            pltpu.SMEM((16, slots), I32),
+            pltpu.SemaphoreType.DMA,
+        ],
+        compiler_params=pltpu.CompilerParams(vmem_limit_bytes=20 << 20),
+        name="score",
+    )(every, passages, lists, ranks, owners)
+
+
+def return_kernel(
+    count, acc, partial, ranks, owners, pairs_q, pairs_p, cand_ref, spots, out, total, compact, slabs, send, recv
+):
+    me = lax.axis_index("shard")
+    block, ids = cand_ref.shape
+    arrive = meet(me, count)
+    total[...] = partial[...]
+    for j in range(EARLY):
+        spread(j, acc, ranks, owners, total, acc.shape[1] // 8)
 
     def pack(i, _):
         rows = total[pl.ds(pl.multiple_of(i * block, block), block), :]
@@ -431,38 +470,11 @@
         both = jnp.concatenate([high, (rows - high.astype(F32)).astype(BF16)], axis=0)
         found = jnp.dot(both, pairs_p[i], preferred_element_type=F32)
         found = (found[:block] + found[block:]) * pairs_q[i].astype(F32)
-        out[i] = jnp.sum(found, axis=0, keepdims=True)
+        compact[i] = jnp.sum(found, axis=0, keepdims=True)
         return 0
 
     lax.fori_loop(0, count, pack, 0, unroll=8)
-
-
-def score(every, passages, lists, ranks, owners, pairs_q, pairs_p):
-    qcount, qtok, _ = every.shape
-    pcount = passages.shape[0]
-    slots = lists.shape[1]
-    vmem = pl.BlockSpec(memory_space=pltpu.VMEM)
-    return pl.pallas_call(
-        score_kernel,
-        out_shape=jax.ShapeDtypeStruct((pairs_q.shape[0], 1, ROOM), F32),
-        in_specs=[vmem] * 7,
-        out_specs=vmem,
-        scratch_shapes=[
-            pltpu.VMEM((slots, 8 * qtok), F32),
-            pltpu.VMEM((qcount, pcount), F32),
-            pltpu.SMEM((16, slots), I32),
-            pltpu.SemaphoreType.DMA,
-        ],
-        compiler_params=pltpu.CompilerParams(vmem_limit_bytes=20 << 20),
-        name="score",
-    )(every, passages, lists, ranks, owners, pairs_q, pairs_p)
-
-
-def return_kernel(count, pcount, compact, cand_ref, spots, out, slabs, send, recv):
-    me = lax.axis_index("shard")
-    block, ids = cand_ref.shape
-    arrive = meet(me, count)
-    owner, _ = place_of(cand_ref[...], pcount)
+    owner, _ = place_of(cand_ref[...], partial.shape[1])
     spot = spots[...]
     spot_w = jnp.concatenate([spot % LANES] * (LANES // ids), axis=1)
     arrive()
@@ -497,27 +509,36 @@
     out[...] = result
 
 
-def give_back(compact, candidates, spots, pcount):
+def give_back(acc, partial, ranks, owners, pairs_q, pairs_p, candidates, spots):
     block, ids = candidates.shape
-    count = compact.shape[0]
+    count = pairs_q.shape[0]
     vmem = pl.BlockSpec(memory_space=pltpu.VMEM)
     dma = pltpu.SemaphoreType.DMA
     return pl.pallas_call(
-        functools.partial(return_kernel, count, pcount),
+        functools.partial(return_kernel, count),
         out_shape=jax.ShapeDtypeStruct((block, ids), F32),
-        in_specs=[vmem] * 3,
+        in_specs=[vmem] * 8,
         out_specs=vmem,
-        scratch_shapes=[pltpu.VMEM((count, 1, ROOM), F32), dma((count,)), dma((count,))],
+        scratch_shapes=[
+            pltpu.VMEM(partial.shape, F32),
+            pltpu.VMEM((count, 1, ROOM), F32),
+            pltpu.VMEM((count, 1, ROOM), F32),
+            dma((count,)),
+            dma((count,)),
+        ],
         compiler_params=pltpu.CompilerParams(collective_id=1, has_side_effects=True, vmem_limit_bytes=8 << 20),
         name="give_back",
-    )(compact, candidates, spots)
+    )(acc, partial, ranks, owners, pairs_q, pairs_p, candidates, spots)
 
 
 def shards(queries, passages, lengths, candidates):
     count = lax.axis_size("shard")
     tokens_first = jnp.swapaxes(passages, 0, 1)
-    *made, spots = gather(queries, candidates, tokens_first, lengths.reshape(1, -1), count)
-    return give_back(score(*made), candidates, spots, passages.shape[0])
+    every, kept, lists, ranks, owners, pairs_q, pairs_p, spots = gather(
+        queries, candidates, tokens_first, lengths.reshape(1, -1), count
+    )
+    best, partial = score(every, kept, lists, ranks, owners)
+    return give_back(best, partial, ranks, owners, pairs_q, pairs_p, candidates, spots)
 
 
 def solution(mesh):

time: 49.4 us -> 46.6 us (0.943); the launches traced: 49.4 us -> 45.7 us
  Pallas kernels: 48.7 us -> 45.1 us
    pallas_call x2, Pallas kernels: 22.3 us -> 19.4 us  [the longest x1 12 us: give_back(): pl.pallas_call(functools.partial(return_kernel, count), out_shape=jax.Sha...]
    pallas_call x1, Pallas kernels: 26.4 us -> 25.7 us  [gather(): pl.pallas_call(functools.partial(gather_kernel, count), out_shape=(jax.Sh...]
where the time goes in v4:
time: 46.6 us; the launch traced here: 45.7 us
  Pallas kernels  45.1 us (97%)
  local copies, waits for them, and re-layouts  0.61 us (1%)
    pallas_call x1, Pallas kernels, gather(): pl.pallas_call(functools.partial(gather_kernel, count), out_shape=(jax.Sh...  25.7 us
    pallas_call x1, Pallas kernels, give_back(): pl.pallas_call(functools.partial(return_kernel, count), out_shape=jax.Sha...  12 us
    pallas_call x1, Pallas kernels, score(): pl.pallas_call(score_kernel, out_shape=(jax.ShapeDtypeStruct((slots, 8 *...  7.36 us

profile of v4, /device:TPU:1, one launch (start us, length us, event | category | flops | bytes accessed | tf_op | source)
XLA Modules:
  0.0 45.7 jit_solution(10961659847578321342)
XLA Ops:
  0.0 25.7 %gather.1 = (bf16[512,32,128]{2,1,0:T(8,128)(2,1)S(1)}, bf16[128,180,128]{2,1,0:T(8,128)(2,1)S(1)}, s32[16,896]{1,0:T(8,128)S(1)}, f32[7,512,128]{2,1,0:T(8,128)...) custom-call(bf16[16,32,128]{2,1,0:T(8,128)(2,1)} %q_ref.1, ...), custom_call_target="tpu_custom_call" | custom-call | tf_op jit(solution)/shard_map/gather/pallas_call | solution.py:351
  25.7 0.0 copy-start
  25.7 7.4 %score.1 = (f32[896,256]{1,0:T(8,128)S(1)}, f32[512,128]{1,0:T(8,128)S(1)}) custom-call(bf16[512,32,128]{2,1,0:T(8,128)(2,1)S(1)} %get-tuple-element.15.qall, bf16[128,180,128]{2,1,0:T(8,128)(2,1)S(1)} %get-tuple-element.16.pbuf, s32[16,896]{1,0:T(8,128)S(1)} %get-tuple-element.17.lists, f32[7,512,128]{2,1,0:T(8,128)S(1)} %get-tuple-element.18.ranks, ...), custom_call_target="tpu_custom_call" | custom-call | tf_op jit(solution)/shard_map/score/pallas_call | solution.py:440
  33.1 0.0 copy-done
  33.1 12.0 %give_back.1 = f32[16,64]{1,0:T(8,128)S(1)} custom-call(f32[896,256]{1,0:T(8,128)S(1)} %get-tuple-element.20.acc, f32[512,128]{1,0:T(8,128)S(1)} %get-tuple-element.21.partial, f32[7,512,128]{2,1,0:T(8,128)S(1)} %get-tuple-element.18.ranks, bf16[7,128,128]{2,1,0:T(8,128)(2,1)S(1)} %get-tuple-element.19.owners, ...), custom_call_target="tpu_custom_call" | custom-call | tf_op jit(solution)/shard_map/give_back/pallas_call | solution.py:517
  45.1 0.6 %copy.6 = f32[16,64]{1,0:T(8,128)} copy(f32[16,64]{1,0:T(8,128)S(1)} %give_back.1) | data formatting | bytes 8192
Async XLA Ops:
  25.7 7.4 %copy-start = (s32[16,64]{1,0:T(8,128)S(1)}, s32[16,64]{1,0:T(8,128)}, u32[]{:S(2)}) copy-start(s32[16,64]{1,0:T(8,128)} %cand_ref.3) | copy-start | bytes 12292

commit v5 on v4

--- a/solution.py
+++ b/solution.py
@@ -35,7 +35,7 @@
         pl.semaphore_signal(barrier, inc=1, device_id={"shard": (me + k) % count}, device_id_type=MESH)
         return 0
 
-    lax.fori_loop(1, count, tell, 0)
+    lax.fori_loop(1, count, tell, 0, unroll=True)
     return lambda: pl.semaphore_wait(barrier, count - 1)
 
 
@@ -136,7 +136,7 @@
             action(slab_copy(k))
             return 0
 
-        lax.fori_loop(1, count, go, 0)
+        lax.fori_loop(1, count, go, 0, unroll=True)
 
     full, low, high = (0, part), (0, part // 2), (part // 2, part // 2)
     halves = (0, 1)
@@ -206,7 +206,7 @@
             pbuf[pl.ds(p, 16), pl.ds(t, 16), :] = jnp.swapaxes(stage[pl.ds(t, 16), pl.ds(p, 16), :], 0, 1)
             return 0
 
-        lax.fori_loop(0, plen // 16 * (phalf // 16), go, 0)
+        lax.fori_loop(0, plen // 16 * (phalf // 16), go, 0, unroll=4)
         rest = plen // 16 * 16
         if rest < plen:
             for i in range(phalf // 16):
@@ -390,9 +390,18 @@
 def score_kernel(qall, pbuf, lists, ranks, owners, acc, total, table, sem):
     qcount, qtok, dim = qall.shape
     pcount, plen, _ = pbuf.shape
-    move = pltpu.make_async_copy(lists, table, sem)
+    first = EARLY * LANES + UNROLL
+    first = (first + LANES - 1) // LANES * LANES
+    move = pltpu.make_async_copy(lists.at[:, :first], table.at[:, :first], sem)
     move.start()
     move.wait()
+
+    @pl.when(table[9 + len(BOUNDS), 0] + UNROLL > first)
+    def _():
+        rest = pltpu.make_async_copy(lists.at[:, first:], table.at[:, first:], sem)
+        rest.start()
+        rest.wait()
+
     start = 0
     for c, rows in enumerate(BOUNDS + (plen,)):
         end = table[9 + c, 0]
@@ -495,7 +504,7 @@
             action(slab_copy(k))
             return 0
 
-        lax.fori_loop(1, count, go, 0)
+        lax.fori_loop(1, count, go, 0, unroll=True)
 
     each(lambda copy: copy.start())
     slabs[me] = compact[me]

time: 46.6 us -> 45.7 us (0.981); the launches traced: 45.7 us -> 45.6 us
  no operation moved by 1% of the time
where the time goes in v5:
time: 45.7 us; the launch traced here: 45.6 us
  Pallas kernels  45 us (98%)
  local copies, waits for them, and re-layouts  0.61 us (1%)
    pallas_call x1, Pallas kernels, gather(): pl.pallas_call(functools.partial(gather_kernel, count), out_shape=(jax.Sh...  25.5 us
    pallas_call x1, Pallas kernels, give_back(): pl.pallas_call(functools.partial(return_kernel, count), out_shape=jax.Sha...  12.5 us
    pallas_call x1, Pallas kernels, score(): pl.pallas_call(score_kernel, out_shape=(jax.ShapeDtypeStruct((slots, 8 *...  6.96 us

profile of v5, /device:TPU:1, one launch (start us, length us, event | category | flops | bytes accessed | tf_op | source)
XLA Modules:
  0.0 45.6 jit_solution(11769101546383904005)
XLA Ops:
  0.0 25.5 %gather.1 = (bf16[512,32,128]{2,1,0:T(8,128)(2,1)S(1)}, bf16[128,180,128]{2,1,0:T(8,128)(2,1)S(1)}, s32[16,896]{1,0:T(8,128)S(1)}, f32[7,512,128]{2,1,0:T(8,128)...) custom-call(bf16[16,32,128]{2,1,0:T(8,128)(2,1)} %q_ref.1, ...), custom_call_target="tpu_custom_call" | custom-call | tf_op jit(solution)/shard_map/gather/pallas_call | solution.py:351
  25.5 0.0 copy-start
  25.6 7.0 %score.1 = (f32[896,256]{1,0:T(8,128)S(1)}, f32[512,128]{1,0:T(8,128)S(1)}) custom-call(bf16[512,32,128]{2,1,0:T(8,128)(2,1)S(1)} %get-tuple-element.15.qall, bf16[128,180,128]{2,1,0:T(8,128)(2,1)S(1)} %get-tuple-element.16.pbuf, s32[16,896]{1,0:T(8,128)S(1)} %get-tuple-element.17.lists, f32[7,512,128]{2,1,0:T(8,128)S(1)} %get-tuple-element.18.ranks, ...), custom_call_target="tpu_custom_call" | custom-call | tf_op jit(solution)/shard_map/score/pallas_call | solution.py:449
  32.5 0.0 copy-done
  32.5 12.5 %give_back.1 = f32[16,64]{1,0:T(8,128)S(1)} custom-call(f32[896,256]{1,0:T(8,128)S(1)} %get-tuple-element.20.acc, f32[512,128]{1,0:T(8,128)S(1)} %get-tuple-element.21.partial, f32[7,512,128]{2,1,0:T(8,128)S(1)} %get-tuple-element.18.ranks, bf16[7,128,128]{2,1,0:T(8,128)(2,1)S(1)} %get-tuple-element.19.owners, ...), custom_call_target="tpu_custom_call" | custom-call | tf_op jit(solution)/shard_map/give_back/pallas_call | solution.py:526
  45.0 0.6 %copy.6 = f32[16,64]{1,0:T(8,128)} copy(f32[16,64]{1,0:T(8,128)S(1)} %give_back.1) | data formatting | bytes 8192
Async XLA Ops:
  25.5 7.0 %copy-start = (s32[16,64]{1,0:T(8,128)S(1)}, s32[16,64]{1,0:T(8,128)}, u32[]{:S(2)}) copy-start(s32[16,64]{1,0:T(8,128)} %cand_ref.3) | copy-start | bytes 12292
